TPU v7x, 512 devices: a whole 4x8x8 slice. The times are simulated.
512 devices in a mesh: half: 2 (over x_lo), grid: 8 (over y), dom: 32 (over z, x_hi, core).
Axes of the slice: x: 4 (x_hi: 2, x_lo: 2; x = x_hi * 2 + x_lo), y: 8, z: 8, core: 2. Of those that a mesh axis runs over, the one named last changes fastest.
Arguments:
- grids: float32 [16, 64, 64, 4096], P(('half', 'grid'), 'dom'), may hold values from -0.8 to 0.8
- levels: int32 [16, 4], replicated, may hold values from 4 to 6, as said below
Outputs:
- combined: float32 [16, 64, 64, 4096], P(('half', 'grid'), 'dom')
Inputs may be any that keep to these rules, and one draw needn't show every extreme that they name: `levels`: with base b = (4, 5, 5, 5), rows 0 to 7 are b plus, in some order, (2,1,1,0), (2,1,0,1), (2,0,1,1), (1,1,1,1), (1,1,0,0), (1,0,1,0), (1,0,0,1), (0,0,0,0); rows 8 to 15 are b plus, in some order, (2,1,0,0), (2,0,1,0), (2,0,0,1), (1,1,1,0), (1,1,0,1), (1,0,1,1), (2,0,0,0), (1,0,0,0).
All inputs are finite; a program needn't handle non-finite values.
Results may differ from a plain program's by a relative error of at most 0.0003.
Values sent between devices are 32-bit elements; how exact they have to be, the bound alone decides.
A program may use at most 128 MiB of HBM per device.

v0:
```python
import jax
import jax.numpy as jnp
import numpy as np
from jax import lax
from jax.sharding import PartitionSpec as P

LEV1 = 6
LEV2 = 6
LEV3 = 6
LEV4 = 6
N1 = 64
N2 = 64
N3 = 64
N4 = 64


HIGH = lax.Precision.HIGHEST
SPANS = (2, 1, 1, 1)


def level_ordering(level):
    points = 2**level
    ordering = [0]
    for section in range(1, level + 1):
        stride = 2 ** (level - section)
        ordering.extend(range(stride, points, 2 * stride))
    return np.array(ordering)


def hier_tables(level_top, spread):
    size_top = 2**level_top
    forwards = np.zeros((spread + 1, size_top, size_top))
    backwards = np.zeros((spread + 1, size_top, size_top))
    for offset in range(spread + 1):
        level = level_top - spread + offset
        points = 2**level
        down_rows = np.eye(points)
        up_rows = np.eye(points)
        for section in range(level, 0, -1):
            stride = 2 ** (level - section)
            odd_points = np.arange(stride, points, 2 * stride)
            down_rows[odd_points] = down_rows[odd_points] - 0.5 * (
                down_rows[odd_points - stride] + down_rows[(odd_points + stride) % points]
            )
        for section in range(1, level + 1):
            stride = 2 ** (level - section)
            odd_points = np.arange(stride, points, 2 * stride)
            up_rows[odd_points] = up_rows[odd_points] + 0.5 * (
                up_rows[odd_points - stride] + up_rows[(odd_points + stride) % points]
            )
        ordering = level_ordering(level)
        forwards[offset, :points, :points] = down_rows[ordering]
        backwards[offset, :points, :points] = up_rows[:, ordering]
    return (jnp.asarray(forwards, jnp.float32), jnp.asarray(backwards, jnp.float32))


def combination_weights(levels):
    corners = np.array(
        [[corner >> place & 1 for place in range(4)] for corner in range(16)], dtype=np.int32
    )
    parity = 1 - 2 * (corners.sum(axis=1) % 2)
    raised = levels[:, None, :] + jnp.asarray(corners, dtype=jnp.int32)[None, :, :]
    below = jnp.all(raised[:, :, None, :] <= levels[None, None, :, :], axis=3)
    inside = jnp.any(below, axis=2).astype(jnp.int32)
    return jnp.sum(inside * jnp.asarray(parity, dtype=jnp.int32)[None, :], axis=1)


def pick_tables(tables, level_column, level_top, spread):
    shifted = level_column - (level_top - spread)
    onehot = (jnp.arange(spread + 1, dtype=jnp.int32)[None, :] == shifted[:, None]).astype(
        jnp.float32
    )
    return jnp.einsum("gs,sij->gij", onehot, tables, precision=HIGH)


def block_cover(levels, upper_block):
    lowest = jnp.array([LEV1 - 2, LEV2 - 1, LEV3 - 1, LEV4 - 1], dtype=jnp.int32)
    offsets = levels - lowest[None, :]
    blocks = jnp.arange(16, dtype=jnp.int32)
    first_block = jnp.minimum(blocks // 4, 2)
    third_block = blocks // 2 % 2
    fourth_block = blocks % 2
    covered = first_block[None, :] <= offsets[:, 0:1]
    covered = covered & (upper_block <= offsets[:, 1:2])
    covered = covered & (third_block[None, :] <= offsets[:, 2:3])
    return covered & (fourth_block[None, :] <= offsets[:, 3:4])


def compact_order(mask):
    ranking = jnp.argsort(jnp.where(mask, 0, 16) + jnp.arange(16, dtype=jnp.int32))
    return (ranking, mask[ranking].astype(jnp.float32))


def pick_rows(blocks, order, valid):
    return jnp.take(blocks, order, axis=0) * valid[:, None]


def place_rows(rows, order, valid):
    return jnp.zeros((16, rows.shape[1]), jnp.float32).at[order].add(rows * valid[:, None])


def combine(blocks, covered):
    order, valid = compact_order(jnp.any(covered, axis=0))
    summed = lax.psum(pick_rows(blocks, order, valid), ("half", "grid"))
    return place_rows(summed, order, valid)


def per_device(grids, levels):
    finest = (LEV1, LEV2, LEV3, LEV4)
    local_count = grids.shape[0]
    rows_here = grids.shape[1]
    grid_count = lax.axis_size("grid")
    group = lax.axis_index("half") * grid_count + lax.axis_index("grid")
    weights = combination_weights(levels).astype(jnp.float32)
    own_levels = lax.dynamic_slice_in_dim(levels, group * local_count, local_count, 0)
    own_weights = lax.dynamic_slice_in_dim(weights, group * local_count, local_count, 0)
    forward_mats = []
    backward_mats = []
    for axis_index in range(4):
        down_tables, up_tables = hier_tables(finest[axis_index], SPANS[axis_index])
        forward_mats.append(
            pick_tables(
                down_tables, own_levels[:, axis_index], finest[axis_index], SPANS[axis_index]
            )
        )
        backward_mats.append(
            pick_tables(up_tables, own_levels[:, axis_index], finest[axis_index], SPANS[axis_index])
        )
    values = grids.reshape(local_count, rows_here, N2, N3, N4)
    values = jnp.einsum("gjl,gabcl->gabcj", forward_mats[3], values, precision=HIGH)
    values = jnp.einsum("gjc,gabcl->gabjl", forward_mats[2], values, precision=HIGH)
    values = jnp.einsum(
        "gjb,gabm->gajm",
        forward_mats[1],
        values.reshape(local_count, rows_here, N2, N3 * N4),
        precision=HIGH,
    )
    surplus = jnp.einsum(
        "gja,gabm->gjbm",
        forward_mats[0],
        lax.all_to_all(values, "dom", split_axis=2, concat_axis=1, tiled=True),
        precision=HIGH,
    )
    scaled = jnp.einsum("g,gjbm->jbm", own_weights, surplus, precision=HIGH)
    pole_rows = scaled.shape[1]
    upper_block = lax.axis_index("dom") * pole_rows // (N2 // 2)
    covered = block_cover(levels, upper_block)
    quarter_rows = N1 // 4
    blocks = (
        scaled.reshape(4, quarter_rows, pole_rows, 2, N3 // 2, 2, N4 // 2)
        .transpose(0, 3, 5, 1, 2, 4, 6)
        .reshape(16, -1)
    )
    summed_blocks = combine(blocks, covered)
    totals = (
        summed_blocks.reshape(4, 2, 2, quarter_rows, pole_rows, N3 // 2, N4 // 2)
        .transpose(0, 3, 4, 1, 5, 2, 6)
        .reshape(N1, pole_rows, N3 * N4)
    )
    expanded = jnp.einsum("gja,abm->gjbm", backward_mats[0], totals, precision=HIGH)
    returned = lax.all_to_all(expanded, "dom", split_axis=1, concat_axis=2, tiled=True)
    returned = jnp.einsum("gjb,gabm->gajm", backward_mats[1], returned, precision=HIGH)
    returned = returned.reshape(local_count, rows_here, N2, N3, N4)
    returned = jnp.einsum("gjc,gabcl->gabjl", backward_mats[2], returned, precision=HIGH)
    returned = jnp.einsum("gjl,gabcl->gabcj", backward_mats[3], returned, precision=HIGH)
    return returned.reshape(local_count, rows_here, N2, N3 * N4)


def solution(mesh):
    return jax.shard_map(
        per_device,
        mesh=mesh,
        in_specs=(P(("half", "grid"), "dom", None, None), P()),
        out_specs=P(("half", "grid"), "dom", None, None),
        check_vma=False,
    )
```

profile of v0, /device:TPU:1, one launch (start us, length us, event | category | flops | bytes accessed | tf_op | source)
XLA Modules:
  0.0 454.5 jit_solution(10062554610760000204)
XLA Ops:
  7.8 4.6 %reshape.191 = f32[2,64,64,64]{3,2,1,0:T(8,128)} reshape(f32[1,2,64,4096]{3,2,1,0:T(8,128)} %param.13) | data formatting | bytes 4194304 | tf_op jit(solution)/shard_map/reshape.17
  14.2 13.8 %fusion.28 = f32[64,2,64,64]{3,0,2,1:T(8,128)S(1)} fusion(f32[64,64,1,1]{1,0,3,2:T(8,128)S(1)} %bitcast.162, f32[2,64,64,64]{3,2,1,0:T(8,128)} %reshape.191), kind=kOutput, calls=%fused_computation.65 | convolution fusion | flops 402653184 | bytes 4210688 | tf_op jit(solution)/shard_map/gjl,gabcl->gabcj/dot_general | solution.py:130
  28.0 4.9 %fusion.4 = f32[1,2,64,64,64]{3,4,2,1,0:T(8,128)} fusion(f32[64,64,1,1]{1,0,3,2:T(8,128)S(1)} %bitcast.161, f32[64,2,64,64]{3,0,2,1:T(8,128)S(1)} %fusion.28), kind=kOutput, calls=%fused_computation.11 | convolution fusion | flops 402653184 | bytes 4210688 | tf_op jit(solution)/shard_map/gjc,gabcl->gabjl/dot_general | solution.py:131
  33.0 5.7 %copy.51 = f32[1,2,64,64,64]{4,3,2,1,0:T(8,128)} copy(f32[1,2,64,64,64]{3,4,2,1,0:T(8,128)} %fusion.4) | data formatting | bytes 4194304 | tf_op jit(solution)/shard_map/gjc,gabcl->gabjl/transpose | solution.py:131
  38.6 3.7 reshape.192
  48.3 14.6 %all-to-all-start = ((f32[1,2,64,4096]{3,1,0,2:T(2,128)}), f32[1,2,64,4096]{3,1,0,2:T(2,128)S(1)}, u32[]{:S(2)}, u32[]{:S(2)}) async-start(f32[1,2,64,4096]{3,1,0,2:T(2,128)} %copy.52), calls=%async_computation | async-start | bytes 4194304 | tf_op jit(solution)/shard_map/all_to_all | solution.py:141
  67.4 45.5 %all-to-all-done = f32[1,2,64,4096]{3,1,0,2:T(2,128)S(1)} async-done(((f32[1,2,64,4096]{3,1,0,2:T(2,128)}), f32[1,2,64,4096]{3,1,0,2:T(2,128)S(1)}, u32[]{:S(2)}, u32[]{:S(2)}) %all-to-all-start) | async-done | bytes 2097184 | tf_op jit(solution)/shard_map/all_to_all | solution.py:141
  114.2 3.3 copy.53
  117.5 3.6 copy.54
  121.1 22.9 %multiply_bitcast_fusion = f32[4,2,2,16,2,32,32]{6,3,2,5,1,4,0:T(8,128)S(1)} fusion(f32[]{:T(128)} %bitcast.9, f32[4,16,64,1,1,1,1]{2,1,6,5,4,3,0:T(8,128)S(1)} %bitcast.157, f32[2,2,32,2,32,64,1]{5,4,3,2,1,0,6:T(8,128)} %bitcast.151), kind=kOutput, calls=%fused_computation.3 | convolution fusion | flops 403177472 | bytes 4210692 | tf_op jit(solution)/shard_map/gja,gabm->gjbm/dot_general | solution.py:138
  144.0 8.0 %copy.55 = f32[4,2,2,16,2,32,32]{6,5,4,3,2,1,0:T(8,128)} copy(f32[4,2,2,16,2,32,32]{6,3,2,5,1,4,0:T(8,128)S(1)} %multiply_bitcast_fusion) | data formatting | bytes 4194304 | tf_op jit(solution)/shard_map/transpose | solution.py:151
  152.0 6.1 %reshape.194 = f32[16,32768]{1,0:T(8,128)S(1)} reshape(f32[4,2,2,16,2,32,32]{6,5,4,3,2,1,0:T(8,128)} %copy.55) | data formatting | bytes 4194304 | tf_op jit(solution)/shard_map/reshape | solution.py:152
  164.8 134.0 %all-reduce.2.cloned.1.call-done = f32[16,32768]{1,0:T(8,128)} async-done(((f32[16,32768]{1,0:T(8,128)}), f32[16,32768]{1,0:T(8,128)}) %all-reduce.2.cloned.1.call-update) | async-done | bytes 2097168 | tf_op jit(solution)/shard_map/psum | solution.py:104
  301.9 4.4 scatter_custom_fusion
  306.2 4.8 %reshape.195 = f32[4,2,2,16,2,32,32]{6,5,4,3,2,1,0:T(8,128)} reshape(f32[16,32768]{1,0:T(8,128)S(1)} %scatter_custom_fusion) | data formatting | bytes 4194304 | tf_op jit(solution)/shard_map/reshape | solution.py:156
  311.0 15.4 %copy.56 = f32[4,16,2,2,32,2,32]{6,5,4,3,1,0,2:T(2,128)} copy(f32[4,16,2,2,32,2,32]{6,4,2,1,5,3,0:T(8,128)} %bitcast.150) | data formatting | bytes 4194304 | tf_op jit(solution)/shard_map/transpose | solution.py:157
  326.4 12.2 %reshape.196 = f32[64,2,4096]{2,0,1:T(8,128)S(1)} reshape(f32[4,16,2,2,32,2,32]{6,5,4,3,1,0,2:T(2,128)} %copy.56) | data formatting | bytes 4194304 | tf_op jit(solution)/shard_map/reshape | solution.py:158
  343.4 20.4 %all-to-all-start.1 = ((f32[1,64,2,4096]{3,2,0,1:T(2,128)}), f32[1,64,2,4096]{3,2,0,1:T(2,128)S(1)}, u32[]{:S(2)}, u32[]{:S(2)}) async-start(f32[1,64,2,4096]{3,2,0,1:T(2,128)} %copy.57), calls=%async_computation.1 | async-start | bytes 4194304 | tf_op jit(solution)/shard_map/all_to_all | solution.py:161
  364.6 49.2 %all-to-all-done.1 = f32[1,64,2,4096]{3,2,0,1:T(2,128)S(1)} async-done(((f32[1,64,2,4096]{3,2,0,1:T(2,128)}), f32[1,64,2,4096]{3,2,0,1:T(2,128)S(1)}, u32[]{:S(2)}, u32[]{:S(2)}) %all-to-all-start.1) | async-done | bytes 2097184 | tf_op jit(solution)/shard_map/all_to_all | solution.py:161
  415.2 3.7 reshape.197
  419.0 3.6 convolution_bitcast_fusion
  425.5 8.6 %fusion.29 = f32[2,64,64,64]{3,2,1,0:T(8,128)S(1)} fusion(f32[2,64,64,64]{3,2,1,0:T(8,128)} %reshape.198, f32[64,64,1,1]{1,0,3,2:T(8,128)S(1)} %bitcast.159), kind=kOutput, calls=%fused_computation.66 | convolution fusion | flops 402653184 | bytes 4210688 | tf_op jit(solution)/shard_map/gjc,gabcl->gabjl/dot_general | solution.py:164
  434.2 8.4 %fusion = f32[2,64,64,64]{3,2,1,0:T(8,128)} fusion(f32[64,64,1,1]{1,0,3,2:T(8,128)S(1)} %bitcast.158, f32[2,64,64,64]{3,2,1,0:T(8,128)S(1)} %fusion.29), kind=kOutput, calls=%fused_computation.7 | convolution fusion | flops 402653184 | bytes 4210688 | tf_op jit(solution)/shard_map/gjl,gabcl->gabcj/dot_general | solution.py:165
  442.6 4.8 %reshape.200 = f32[1,2,64,4096]{3,2,1,0:T(8,128)} reshape(f32[2,64,64,64]{3,2,1,0:T(8,128)} %fusion) | data formatting | bytes 4194304 | tf_op jit(solution)/shard_map/reshape | solution.py:166
  (60 shorter events, 32.1 us)
Async XLA Ops:
  7.8 5.9 %copy-start.8 = (f32[2,64,64]{2,0,1:T(2,128)S(1)}, f32[2,64,64]{2,0,1:T(2,128)}, u32[]{:S(2)}) copy-start(f32[2,64,64]{2,0,1:T(2,128)} %constant.140) | copy-start | bytes 98308
  48.2 14.7 %copy-start.3 = (s32[16,4]{0,1:T(4,128)S(1)}, s32[16,4]{0,1:T(4,128)}, u32[]{:S(2)}) copy-start(s32[16,4]{0,1:T(4,128)} %param.14) | copy-start | bytes 772
  48.2 14.8 %copy-start.4 = (s32[16,4]{0,1:T(4,128)S(1)}, s32[16,4]{0,1:T(4,128)}, u32[]{:S(2)}) copy-start(s32[16,4]{0,1:T(4,128)} %constant.129.clone) | copy-start | bytes 772
  48.2 15.4 %copy-start.6 = (s32[16]{0:T(128)S(1)}, s32[16]{0:T(128)}, u32[]{:S(2)}) copy-start(s32[16]{0:T(128)} %constant.130.clone) | copy-start | bytes 196
  48.2 16.2 %copy-start.5 = (s32[4]{0:T(128)S(1)}, s32[4]{0:T(128)}, u32[]{:S(2)}) copy-start(s32[4]{0:T(128)} %constant.137) | copy-start | bytes 52
  48.2 18.9 %copy-start.2 = (f32[3,64,64]{2,0,1:T(4,128)S(1)}, f32[3,64,64]{2,0,1:T(4,128)}, u32[]{:S(2)}) copy-start(f32[3,64,64]{2,0,1:T(4,128)} %constant.139) | copy-start | bytes 147460
  48.3 64.7 %all-to-all-start = ((f32[1,2,64,4096]{3,1,0,2:T(2,128)}), f32[1,2,64,4096]{3,1,0,2:T(2,128)S(1)}, u32[]{:S(2)}, u32[]{:S(2)}) async-start(f32[1,2,64,4096]{3,1,0,2:T(2,128)} %copy.52), calls=%async_computation | async-start | bytes 4194304 | tf_op jit(solution)/shard_map/all_to_all | solution.py:141
  62.8 235.9 %all-reduce.2.cloned.1.call-start = ((), (), s32[]{:S(2)}) async-start(), calls=%async_computation.2 | async-start | bytes 4194304 | tf_op jit(solution)/shard_map/psum | solution.py:104
  112.9 1.3 copy-start
  163.6 0.9 copy-start.1
  343.4 20.4 %copy-start.7 = (f32[2,64,64]{2,0,1:T(2,128)S(1)}, f32[2,64,64]{2,0,1:T(2,128)}, u32[]{:S(2)}) copy-start(f32[2,64,64]{2,0,1:T(2,128)} %constant.141) | copy-start | bytes 98308
  343.4 70.3 %all-to-all-start.1 = ((f32[1,64,2,4096]{3,2,0,1:T(2,128)}), f32[1,64,2,4096]{3,2,0,1:T(2,128)S(1)}, u32[]{:S(2)}, u32[]{:S(2)}) async-start(f32[1,64,2,4096]{3,2,0,1:T(2,128)} %copy.57), calls=%async_computation.1 | async-start | bytes 4194304 | tf_op jit(solution)/shard_map/all_to_all | solution.py:161
Sparse Core Ops, SparseCore 0:
  163.8 134.9 all-reduce.1
where the time goes:
time: 461 us; the launch traced here: 455 us
  waiting for transfers between devices  229 us (50%)
  local copies, waits for them, and re-layouts  93.4 us (20%)
  matrix products  68.2 us (15%)
  starting transfers between devices  35 us (8%)
  between operations  16.5 us (4%)
  other arithmetic  12.8 us (3%)
    psum x1, waiting for transfers between devices, combine(): summed = lax.psum(pick_rows(blocks, order, valid), ('half', 'grid'))  134 us
    all_to_all x1, waiting for transfers between devices, per_device(): lax.all_to_all(expanded, 'dom', split_axis=1, concat_axis=2, tiled=True)  49.2 us
    all_to_all x1, waiting for transfers between devices, per_device(): lax.all_to_all(values, 'dom', split_axis=2, concat_axis=1, tiled=True)  45.5 us
    dot_general x1, matrix products, per_device(): jnp.einsum('gja,gabm->gjbm', forward_mats[0], lax.all_to_all(values, 'dom...  22.9 us
    all_to_all x1, starting transfers between devices, per_device(): lax.all_to_all(expanded, 'dom', split_axis=1, concat_axis=2, tiled=True)  20.4 us
    transpose x1, local copies, waits for them, and re-layouts, per_device(): totals = summed_blocks.reshape(4, 2, 2, quarter_rows, pole_rows, N3 // 2,...  15.4 us
    another operation x4, local copies, waits for them, and re-layouts  15.1 us
    all_to_all x1, starting transfers between devices, per_device(): lax.all_to_all(values, 'dom', split_axis=2, concat_axis=1, tiled=True)  14.6 us
  transfers between devices with their start and end apart: 3, of which 3 were waited for; matrix products, arithmetic and copies ran while one was open for 1% of the time, Pallas kernels for 0%

commit v1 on v0

v1 whole, which is shorter than its diff:
```python
import jax
import jax.numpy as jnp
import numpy as np
from jax import lax
from jax.experimental import pallas as pl
from jax.experimental.pallas import tpu as pltpu
from jax.sharding import PartitionSpec as P

LEV1 = 6
LEV2 = 6
LEV3 = 6
LEV4 = 6
MESH = pl.DeviceIdType.MESH
LOWEST = (LEV1 - 2, LEV2 - 1, LEV3 - 1, LEV4 - 1)


def combination_weights(levels):
    corners = np.array(
        [[corner >> place & 1 for place in range(4)] for corner in range(16)], dtype=np.int32
    )
    parity = 1 - 2 * (corners.sum(axis=1) % 2)
    raised = levels[:, None, :] + jnp.asarray(corners, dtype=jnp.int32)[None, :, :]
    below = jnp.all(raised[:, :, None, :] <= levels[None, None, :, :], axis=3)
    inside = jnp.any(below, axis=2).astype(jnp.int32)
    return jnp.sum(inside * jnp.asarray(parity, dtype=jnp.int32)[None, :], axis=1)


def lift_tables():
    down = np.zeros((2, 64, 64))
    up = np.zeros((2, 64, 64))
    for p in range(32):
        down[0, p, p] = 1
        up[0, p, p] = 1
        after = (p + 1) % 32
        down[1, p, 2 * p] = 1
        down[1, 32 + p, 2 * p + 1] = 1
        down[1, 32 + p, 2 * p] -= 0.5
        down[1, 32 + p, 2 * after] -= 0.5
        up[1, 2 * p, p] = 1
        up[1, 2 * p + 1, 32 + p] = 1
        up[1, 2 * p + 1, p] += 0.5
        up[1, 2 * p + 1, after] += 0.5
    return down, up


def row_tables():
    down, up = lift_tables()
    forward = np.zeros((2, 128, 128))
    backward = np.zeros((2, 128, 128))
    for a in range(2):
        for k in range(64):
            row = (k // 4) * 8 + a * 4 + k % 4
            forward[:, row, a * 64 : a * 64 + 64] = down[:, k, :]
            backward[:, a * 64 : a * 64 + 64, row] = up[:, :, k]
    return jnp.asarray(forward, jnp.bfloat16), jnp.asarray(backward, jnp.bfloat16)


def lane_tables():
    down, up = lift_tables()
    forward = np.zeros((2, 4, 2, 64, 2, 2, 4, 32))
    backward = np.zeros((2, 2, 2, 4, 32, 4, 2, 64))
    for parity in range(2):
        for j in range(4):
            for high in range(2):
                rows = slice(32 * high, 32 * high + 32)
                forward[:, j, parity, :, parity, high, j, :] = down[:, rows, :].transpose(0, 2, 1)
                backward[:, parity, high, j, :, j, parity, :] = up[:, :, rows].transpose(0, 2, 1)
    return (
        jnp.asarray(forward.reshape(2, 512, 512), jnp.bfloat16),
        jnp.asarray(backward.reshape(2, 512, 512), jnp.bfloat16),
    )


def split(values):
    high = values.astype(jnp.bfloat16)
    low = (values - high.astype(jnp.float32)).astype(jnp.bfloat16)
    return high, low


def dot(left, right):
    return jnp.dot(left, right, preferred_element_type=jnp.float32)


def roll_lanes(values):
    return jnp.concatenate(
        [pltpu.roll(values[:, :128], 96, 1), pltpu.roll(values[:, 128:], 96, 1)], axis=1
    )


def forward_kernel(meta_ref, x_ref, lane_ref, row_ref, send_ref, held):
    c_high = meta_ref[1]
    count = 4 + 4 * c_high

    def step(i, _):
        tiles = [
            x_ref[:, pl.ds(pl.multiple_of((i + j * count) * 128, 128), 128)] for j in range(4)
        ]
        high, low = split(jnp.concatenate(tiles, axis=1))
        lane = lane_ref[0]
        out = dot(high, lane) + dot(low, lane)
        held[jnp.where(c_high == 1, i, 2 * i)] = out[:, :256]
        held[jnp.where(c_high == 1, 8 + i, 2 * i + 1)] = out[:, 256:]
        return 0

    lax.fori_loop(0, count, step, 0)

    @pl.when(c_high == 1)
    def _():
        for m in range(8):
            after = held[m + 1] if m < 7 else roll_lanes(held[0])
            held[8 + m] = held[8 + m] - 0.5 * (held[m] + after)

    def rows(i, _):
        high, low = split(held[i])
        row = row_ref[0]
        out = dot(row, high) + dot(row, low)
        c = i // 8
        m = i % 8
        for b in range(2):
            for d in range(2):
                block = b * 4 + c * 2 + d

                @pl.when(meta_ref[12 + block] == 1)
                def _():
                    slot = meta_ref[4 + block]
                    for half in range(2):
                        start = b * 64 + half * 32
                        send_ref[half * 8 + m, slot] = out[
                            start : start + 32, d * 128 : d * 128 + 128
                        ]

        return 0

    lax.fori_loop(0, 8 + 8 * c_high, rows, 0)


def backward_kernel(meta_ref, recv_ref, lane_ref, row_ref, out_ref, held):
    c_high = meta_ref[1]
    count = 4 + 4 * c_high

    @pl.when(meta_ref[3] == 0)
    def _():
        out_ref[...] = jnp.zeros_like(out_ref)

    @pl.when(meta_ref[3] == 1)
    def _():
        def rows(i, _):
            c = i // 8
            m = i % 8
            columns = []
            for d in range(2):
                parts = []
                for b in range(2):
                    block = b * 4 + c * 2 + d
                    slot = meta_ref[4 + block]
                    covered = meta_ref[12 + block] == 1
                    for half in range(2):
                        part = recv_ref[half * 8 + m, slot]
                        parts.append(jnp.where(covered, part, 0.0))
                columns.append(jnp.concatenate(parts, axis=0))
            high, low = split(jnp.concatenate(columns, axis=1))
            row = row_ref[0]
            held[i] = dot(row, high) + dot(row, low)
            return 0

        lax.fori_loop(0, 8 + 8 * c_high, rows, 0)

        @pl.when(c_high == 1)
        def _():
            for m in range(8):
                after = held[m + 1] if m < 7 else roll_lanes(held[0])
                held[8 + m] = held[8 + m] + 0.5 * (held[m] + after)

        def step(i, _):
            even = held[jnp.where(c_high == 1, i, 2 * i)]
            odd = held[jnp.where(c_high == 1, 8 + i, 2 * i + 1)]
            high, low = split(jnp.concatenate([even, odd], axis=1))
            lane = lane_ref[0]
            out = dot(high, lane) + dot(low, lane)
            for j in range(4):
                out_ref[:, pl.ds(pl.multiple_of((i + j * count) * 128, 128), 128)] = out[
                    :, j * 128 : j * 128 + 128
                ]
            return 0

        lax.fori_loop(0, count, step, 0)

        @pl.when(c_high == 0)
        def _():
            out_ref[:, 2048:] = jnp.zeros((128, 2048), jnp.float32)


def exchange_kernel(
    slot_ref,
    coef_ref,
    pick_ref,
    send_ref,
    out_ref,
    r1,
    acc,
    r2,
    o2,
    r3,
    s2,
    send1,
    recv1,
    send2,
    recv2,
    send2c,
    recv2c,
    send3,
    recv3,
    send3c,
    recv3c,
    send4,
    recv4,
    own,
):
    half = lax.axis_index("half")
    me = half * 8 + lax.axis_index("grid")
    dom = lax.axis_index("dom")
    far = dom // 16

    for s in range(8):
        r2[s, 2] = jnp.zeros((8, 128), jnp.float32)

    barrier = pltpu.get_barrier_semaphore()

    def greet_group(k, _):
        peer = (me + k) % 16
        pl.semaphore_signal(
            barrier, inc=1, device_id={"half": peer // 8, "grid": peer % 8}, device_id_type=MESH
        )
        return 0

    def greet_dom(k, _):
        pl.semaphore_signal(
            barrier, inc=1, device_id={"dom": (dom + k) % 32}, device_id_type=MESH
        )
        return 0

    lax.fori_loop(1, 16, greet_group, 0)
    lax.fori_loop(1, 32, greet_dom, 0)
    pl.semaphore_wait(barrier, 46)

    def sized(key, act):
        for option in range(3):

            @pl.when(key == option)
            def _():
                act(8 >> option)

    def copy1(source, peer, count):
        return pltpu.make_async_remote_copy(
            src_ref=send_ref.at[peer, pl.ds(0, count)],
            dst_ref=r1.at[source, pl.ds(0, count)],
            send_sem=send1.at[peer],
            recv_sem=recv1.at[source],
            device_id={"half": peer // 8, "grid": peer % 8},
            device_id_type=MESH,
        )

    def start1(k, _):
        peer = (me + k) % 16
        sized(half + far, lambda count: copy1(me, peer, count).start())
        return 0

    lax.fori_loop(1, 16, start1, 0)

    def wait1(k, _):
        source = (me + 16 - k) % 16
        sized(source // 8 + far, lambda count: copy1(source, source, count).wait_recv())
        return 0

    lax.fori_loop(1, 16, wait1, 0)

    def first(block, _):
        slot = slot_ref[me * 8 + block]
        base = (me * 8 + block) * 3
        for group in range(4):
            value = send_ref[me, slot, pl.ds(group * 8, 8), :]
            for kind in range(3):
                acc[block * 4 + group, kind] = value * coef_ref[base + kind]
        return 0

    lax.fori_loop(0, 8, first, 0)

    def add(i, _):
        source = (me + 1 + i // 8) % 16
        block = i % 8
        slot = slot_ref[source * 8 + block]
        base = (source * 8 + block) * 3
        for group in range(4):
            value = r1[source, slot, pl.ds(group * 8, 8), :]
            for kind in range(3):
                acc[block * 4 + group, kind] += value * coef_ref[base + kind]
        return 0

    lax.fori_loop(0, 120, add, 0)

    def copy2(source, peer, count):
        return pltpu.make_async_remote_copy(
            src_ref=acc.at[peer, pl.ds(0, count)],
            dst_ref=r2.at[source, pl.ds(0, count)],
            send_sem=send2.at[peer],
            recv_sem=recv2.at[source],
            device_id={"dom": peer},
            device_id_type=MESH,
        )

    def copy2c(source, peer):
        return pltpu.make_async_remote_copy(
            src_ref=acc.at[peer, pl.ds(2, 1)],
            dst_ref=r2.at[source, pl.ds(2, 1)],
            send_sem=send2c.at[peer],
            recv_sem=recv2c.at[source],
            device_id={"dom": peer},
            device_id_type=MESH,
        )

    def paired(key, act):
        for option in range(2):

            @pl.when(key == option)
            def _():
                act(2 - option)

    def start2(k, _):
        peer = (dom + k) % 32
        paired(far, lambda count: copy2(dom, peer, count).start())

        @pl.when((dom // 8) + (peer // 4) == 0)
        def _():
            copy2c(dom, peer).start()

        return 0

    lax.fori_loop(1, 32, start2, 0)
    for kind in range(2):
        r2[dom, kind] = acc[dom, kind]

    @pl.when(dom // 4 == 0)
    def _():
        r2[dom, 2] = acc[dom, 2]

    def wait2(k, _):
        source = (dom + 32 - k) % 32
        paired(source // 16, lambda count: copy2(source, source, count).wait_recv())

        @pl.when((source // 8) + (dom // 4) == 0)
        def _():
            copy2c(source, source).wait_recv()

        return 0

    lax.fori_loop(1, 32, wait2, 0)

    def part(ref, kind, p):
        return ref[p // 2, kind, (p % 2) * 4 : (p % 2) * 4 + 4, :]

    def put(ref, kind, p, value):
        ref[p // 2, kind, (p % 2) * 4 : (p % 2) * 4 + 4, :] = value

    def joined(p):
        p = p % 32
        return part(r2, 0, 2 * p) + part(r2, 1, p)

    def coarse(q):
        q = q % 16
        return joined(2 * q) + part(r2, 2, q)

    for q in range(16):
        here = coarse(q)
        after = coarse(q + 1)
        middle = joined(2 * q + 1) - 0.5 * (joined(2 * q) + joined(2 * q + 2))
        put(o2, 2, q, here)
        put(o2, 1, 2 * q, here)
        put(o2, 1, 2 * q + 1, middle + 0.5 * (here + after))
    for s in range(32):
        here = part(o2, 1, s)
        after = part(o2, 1, (s + 1) % 32)
        fine = part(r2, 0, 2 * s + 1) - 0.5 * (
            part(r2, 0, 2 * s) + part(r2, 0, (2 * s + 2) % 64)
        )
        put(o2, 0, 2 * s, here)
        put(o2, 0, 2 * s + 1, fine + 0.5 * (here + after))

    def copy3(source, peer, count):
        return pltpu.make_async_remote_copy(
            src_ref=o2.at[peer, pl.ds(0, count)],
            dst_ref=r3.at[pl.ds(source * 3, count)],
            send_sem=send3.at[peer],
            recv_sem=recv3.at[source],
            device_id={"dom": peer},
            device_id_type=MESH,
        )

    def copy3c(source, peer):
        return pltpu.make_async_remote_copy(
            src_ref=o2.at[peer, pl.ds(2, 1)],
            dst_ref=r3.at[pl.ds(source * 3 + 2, 1)],
            send_sem=send3c.at[peer],
            recv_sem=recv3c.at[source],
            device_id={"dom": peer},
            device_id_type=MESH,
        )

    def start3(k, _):
        peer = (dom + k) % 32
        paired(peer // 16, lambda count: copy3(dom, peer, count).start())

        @pl.when((dom // 4) + (peer // 8) == 0)
        def _():
            copy3c(dom, peer).start()

        return 0

    lax.fori_loop(1, 32, start3, 0)
    r3[dom * 3] = o2[dom, 0]

    @pl.when(far == 0)
    def _():
        r3[dom * 3 + 1] = o2[dom, 1]

    @pl.when(dom // 8 == 0)
    def _():
        r3[dom * 3 + 2] = o2[dom, 2]

    def wait3(k, _):
        source = (dom + 32 - k) % 32
        paired(far, lambda count: copy3(source, source, count).wait_recv())

        @pl.when((source // 4) + (dom // 8) == 0)
        def _():
            copy3c(source, source).wait_recv()

        return 0

    lax.fori_loop(1, 32, wait3, 0)

    def fill(peer):
        def one(slot, _):
            pick = pick_ref[peer * 8 + slot]
            for group in range(4):
                s2[peer, slot, pl.ds(group * 8, 8), :] = r3[pick + group * 3]
            return 0

        lax.fori_loop(0, 8, one, 0)

    def copy4(source, peer, count):
        return pltpu.make_async_remote_copy(
            src_ref=s2.at[peer, pl.ds(0, count)],
            dst_ref=out_ref.at[source, pl.ds(0, count)],
            send_sem=send4.at[peer],
            recv_sem=recv4.at[source],
            device_id={"half": peer // 8, "grid": peer % 8},
            device_id_type=MESH,
        )

    def start4(k, _):
        peer = (me + k) % 16
        fill(peer)
        sized(peer // 8 + far, lambda count: copy4(me, peer, count).start())
        return 0

    lax.fori_loop(1, 16, start4, 0)
    fill(me)
    mine = pltpu.make_async_copy(s2.at[me], out_ref.at[me], own)
    mine.start()

    def wait4(k, _):
        source = (me + 16 - k) % 16
        sized(half + far, lambda count: copy4(source, source, count).wait_recv())
        return 0

    lax.fori_loop(1, 16, wait4, 0)
    mine.wait()

    def sent_group(k, _):
        peer = (me + k) % 16
        sized(half + far, lambda count: copy1(me, peer, count).wait_send())
        sized(peer // 8 + far, lambda count: copy4(me, peer, count).wait_send())
        return 0

    lax.fori_loop(1, 16, sent_group, 0)

    def sent_dom(k, _):
        peer = (dom + k) % 32
        paired(far, lambda count: copy2(dom, peer, count).wait_send())
        paired(peer // 16, lambda count: copy3(dom, peer, count).wait_send())

        @pl.when((dom // 8) + (peer // 4) == 0)
        def _():
            copy2c(dom, peer).wait_send()

        @pl.when((dom // 4) + (peer // 8) == 0)
        def _():
            copy3c(dom, peer).wait_send()

        return 0

    lax.fori_loop(1, 32, sent_dom, 0)


def exchange(slots, coefs, picks, packed):
    dma = pltpu.SemaphoreType.DMA
    return pl.pallas_call(
        exchange_kernel,
        out_shape=jax.ShapeDtypeStruct((16, 8, 32, 128), jnp.float32),
        in_specs=[pl.BlockSpec(memory_space=pltpu.SMEM)] * 3
        + [pl.BlockSpec(memory_space=pltpu.VMEM)],
        out_specs=pl.BlockSpec(memory_space=pl.ANY),
        scratch_shapes=[
            pltpu.VMEM((16, 8, 32, 128), jnp.float32),
            pltpu.VMEM((32, 3, 8, 128), jnp.float32),
            pltpu.VMEM((32, 3, 8, 128), jnp.float32),
            pltpu.VMEM((32, 3, 8, 128), jnp.float32),
            pltpu.VMEM((96, 8, 128), jnp.float32),
            pltpu.VMEM((16, 8, 32, 128), jnp.float32),
            dma((16,)),
            dma((16,)),
            dma((32,)),
            dma((32,)),
            dma((32,)),
            dma((32,)),
            dma((32,)),
            dma((32,)),
            dma((32,)),
            dma((32,)),
            dma((16,)),
            dma((16,)),
            dma,
        ],
        compiler_params=pltpu.CompilerParams(
            collective_id=0, has_side_effects=True, vmem_limit_bytes=32 * 2**20
        ),
    )(slots, coefs, picks, packed)


def tables(levels, own, dom):
    offsets = levels - jnp.asarray(LOWEST, dtype=jnp.int32)[None, :]
    first, second, third, fourth = [offsets[:, axis : axis + 1] for axis in range(4)]
    weights = combination_weights(levels)[:, None]
    block = jnp.arange(8, dtype=jnp.int32)[None, :]
    b, c, d = block // 4, block // 2 % 2, block % 2
    covered = (b <= second) & (c <= third) & (d <= fourth)
    slots = jnp.where(covered, (b * (1 + third) + c) * (1 + fourth) + d, 0)
    kind = 2 - first
    reach = (dom < (8 << first)).astype(jnp.int32)
    coefs = (weights * reach * covered.astype(jnp.int32))[:, :, None] * (
        kind[:, :, None] == jnp.arange(3, dtype=jnp.int32)[None, None, :]
    ).astype(jnp.int32)
    d_at = block % (1 + fourth)
    c_at = block // (1 + fourth) % (1 + third)
    b_at = block // ((1 + fourth) * (1 + third))
    chosen = jnp.where(b_at <= second, b_at * 4 + c_at * 2 + d_at, 0)
    picks = chosen * 12 + kind * reach
    meta = jnp.concatenate(
        [second, third, fourth, reach, slots, covered.astype(jnp.int32)], axis=1
    )
    meta = lax.dynamic_slice_in_dim(meta, own, 1, 0).reshape(-1)
    return slots.reshape(-1), coefs.astype(jnp.float32).reshape(-1), picks.reshape(-1), meta


def local_call(kernel, meta, values, block, out_shape, lanes, rows):
    return pl.pallas_call(
        kernel,
        out_shape=jax.ShapeDtypeStruct(out_shape, jnp.float32),
        grid_spec=pltpu.PrefetchScalarGridSpec(
            num_scalar_prefetch=1,
            grid=(1,),
            in_specs=[
                pl.BlockSpec(block, lambda i, meta: (0,) * len(block)),
                pl.BlockSpec((1, 512, 512), lambda i, meta: (meta[2], 0, 0)),
                pl.BlockSpec((1, 128, 128), lambda i, meta: (meta[0], 0, 0)),
            ],
            out_specs=pl.BlockSpec(out_shape, lambda i, meta: (0,) * len(out_shape)),
            scratch_shapes=[pltpu.VMEM((16, 128, 256), jnp.float32)],
        ),
        compiler_params=pltpu.CompilerParams(vmem_limit_bytes=32 * 2**20),
    )(meta, values, lanes, rows)


def per_device(grids, levels):
    own = lax.axis_index("half") * 8 + lax.axis_index("grid")
    slots, coefs, picks, meta = tables(levels, own, lax.axis_index("dom"))
    lane_forward, lane_backward = lane_tables()
    row_forward, row_backward = row_tables()
    packed = local_call(
        forward_kernel,
        meta,
        grids.reshape(128, 4096),
        (128, 4096),
        (16, 8, 32, 128),
        lane_forward,
        row_forward,
    )
    received = exchange(slots, coefs, picks, packed)
    combined = local_call(
        backward_kernel,
        meta,
        received,
        (16, 8, 32, 128),
        (128, 4096),
        lane_backward,
        row_backward,
    )
    return combined.reshape(grids.shape)


def solution(mesh):
    return jax.shard_map(
        per_device,
        mesh=mesh,
        in_specs=(P(("half", "grid"), "dom", None, None), P()),
        out_specs=P(("half", "grid"), "dom", None, None),
        check_vma=False,
    )
```

time: 461 us -> 159 us (0.34)
  the two profiles are of different devices: /device:TPU:1 before, /device:TPU:50 now
where the time goes in v1:
time: 159 us
  Pallas kernels  149 us (94%)
  local copies, waits for them, and re-layouts  4.97 us (3%)
  other arithmetic  4.32 us (3%)
    pallas_call x1, Pallas kernels, exchange(): pl.pallas_call(exchange_kernel, out_shape=jax.ShapeDtypeStruct((16, 8, 32...  135 us
    pallas_call x2, Pallas kernels, local_call(): pl.pallas_call(kernel, out_shape=jax.ShapeDtypeStruct(out_shape, jnp.floa...  14.3 us
    unnamed x11, local copies, waits for them, and re-layouts  4.42 us

profile of v1, /device:TPU:50, one launch (start us, length us, event | category | flops | bytes accessed | tf_op | source)
XLA Modules:
  0.0 158.9 jit_solution(3690257912858539247)
XLA Ops:
  0.0 0.8 broadcast_add_fusion.1
  0.8 0.1 copy.18
  0.9 0.1 copy.19
  1.0 0.8 copy.20
  1.7 0.8 broadcast_add_fusion
  2.5 0.9 compare_reduce_fusion
  3.4 0.3 reduce_or.9
  3.7 0.8 select_reduce_fusion
  4.5 0.1 fusion.11
  4.6 0.1 fusion.27
  4.7 0.4 broadcast_select_fusion
  5.1 0.1 fusion.21.meta_ref
  5.2 0.1 reshape.276.pick_ref
  5.3 0.1 reshape.281.slot_ref
  5.4 0.1 multiply_convert_fusion
  5.5 0.2 convert_element_type.27.coef_ref
  5.7 1.6 copy-done
  7.3 1.2 copy-done.2
  8.5 0.8 copy-done.4
  9.3 6.6 %shard_map.91.send_ref = f32[16,8,32,128]{3,2,1,0:T(8,128)S(1)} custom-call(s32[20]{0:T(128)S(1)} %fusion.21.meta_ref, f32[128,4096]{1,0:T(8,128)S(1)} %bitcast.40, bf16[2,512,512]{2,1,0:T(8,128)(2,1)S(1)} %copy-done.2, bf16[2,128,128]{2,1,0:T(8,128)(2,1)S(1)} %copy-done.4), custom_call_target="tpu_custom_call" | custom-call | tf_op jit(solution)/shard_map/pallas_call | solution.py:566
  16.0 0.0 copy-start.1
  16.0 0.0 copy-start.3
  16.0 135.2 %shard_map.92.recv_ref = f32[16,8,32,128]{3,2,1,0:T(8,128)S(1)} custom-call(s32[128]{0:T(128)S(1)} %reshape.281.slot_ref, f32[384]{0:T(512)S(1)} %convert_element_type.27.coef_ref, s32[128]{0:T(128)S(1)} %reshape.276.pick_ref, f32[16,8,32,128]{3,2,1,0:T(8,128)S(1)} %shard_map.91.send_ref), custom_call_target="tpu_custom_call" | custom-call | tf_op jit(solution)/shard_map/pallas_call | solution.py:507
  151.2 7.7 %shard_map.93 = f32[128,4096]{1,0:T(8,128)} custom-call(s32[20]{0:T(128)S(1)} %fusion.21.meta_ref, f32[16,8,32,128]{3,2,1,0:T(8,128)S(1)} %shard_map.92.recv_ref, bf16[2,512,512]{2,1,0:T(8,128)(2,1)S(1)} %copy-done.1, bf16[2,128,128]{2,1,0:T(8,128)(2,1)S(1)} %copy-done.3), custom_call_target="tpu_custom_call" | custom-call | tf_op jit(solution)/shard_map/pallas_call | solution.py:566
  (11 shorter events, 0.0 us)
Async XLA Ops:
  5.7 1.6 %copy-start = (f32[1,2,64,4096]{3,2,1,0:T(8,128)S(1)}, f32[1,2,64,4096]{3,2,1,0:T(8,128)}, u32[]{:S(2)}) copy-start(f32[1,2,64,4096]{3,2,1,0:T(8,128)} %param.11) | copy-start | bytes 6291460
  7.3 1.2 copy-start.2
  8.5 0.8 copy-start.4
  16.0 135.3 %copy-start.1 = (bf16[2,512,512]{2,1,0:T(8,128)(2,1)S(1)}, bf16[2,512,512]{2,1,0:T(8,128)(2,1)}, u32[]{:S(2)}) copy-start(bf16[2,512,512]{2,1,0:T(8,128)(2,1)} %constant.117.clone.lane_ref) | copy-start | bytes 3145732
  16.0 135.3 %copy-start.3 = (bf16[2,128,128]{2,1,0:T(8,128)(2,1)S(1)}, bf16[2,128,128]{2,1,0:T(8,128)(2,1)}, u32[]{:S(2)}) copy-start(bf16[2,128,128]{2,1,0:T(8,128)(2,1)} %constant.119.clone.row_ref) | copy-start | bytes 196612

commit v2 on v1

v2 whole, which is shorter than its diff:
```python
import jax
import jax.numpy as jnp
import numpy as np
from jax import lax
from jax.experimental import pallas as pl
from jax.experimental.pallas import tpu as pltpu
from jax.sharding import PartitionSpec as P

LEV1 = 6
LEV2 = 6
LEV3 = 6
LEV4 = 6
MESH = pl.DeviceIdType.MESH
LOWEST = (LEV1 - 2, LEV2 - 1, LEV3 - 1, LEV4 - 1)


def lift_tables():
    down = np.zeros((2, 64, 64))
    up = np.zeros((2, 64, 64))
    for p in range(32):
        down[0, p, p] = 1
        up[0, p, p] = 1
        after = (p + 1) % 32
        down[1, p, 2 * p] = 1
        down[1, 32 + p, 2 * p + 1] = 1
        down[1, 32 + p, 2 * p] -= 0.5
        down[1, 32 + p, 2 * after] -= 0.5
        up[1, 2 * p, p] = 1
        up[1, 2 * p + 1, 32 + p] = 1
        up[1, 2 * p + 1, p] += 0.5
        up[1, 2 * p + 1, after] += 0.5
    return down, up


def row_tables():
    down, up = lift_tables()
    forward = np.zeros((2, 128, 128))
    backward = np.zeros((2, 128, 128))
    for a in range(2):
        for k in range(64):
            row = (k // 4) * 8 + a * 4 + k % 4
            forward[:, row, a * 64 : a * 64 + 64] = down[:, k, :]
            backward[:, a * 64 : a * 64 + 64, row] = up[:, :, k]
    return jnp.asarray(forward, jnp.bfloat16), jnp.asarray(backward, jnp.bfloat16)


def lane_tables():
    down, up = lift_tables()
    forward = np.zeros((2, 4, 64, 2, 4, 32))
    backward = np.zeros((2, 2, 4, 32, 4, 64))
    for j in range(4):
        for high in range(2):
            rows = slice(32 * high, 32 * high + 32)
            forward[:, j, :, high, j, :] = down[:, rows, :].transpose(0, 2, 1)
            backward[:, high, j, :, j, :] = up[:, :, rows].transpose(0, 2, 1)
    return (
        jnp.asarray(forward.reshape(2, 256, 256), jnp.bfloat16),
        jnp.asarray(backward.reshape(2, 256, 256), jnp.bfloat16),
    )


def split(values):
    high = values.astype(jnp.bfloat16)
    low = (values - high.astype(jnp.float32)).astype(jnp.bfloat16)
    return high, low


def dot(left, right):
    return jnp.dot(left, right, preferred_element_type=jnp.float32)


def roll_lanes(values):
    return jnp.concatenate(
        [pltpu.roll(values[:, :128], 96, 1), pltpu.roll(values[:, 128:], 96, 1)], axis=1
    )


def swap_halves(first, second):
    front = lax.broadcasted_iota(jnp.int32, first.shape, 1) < 64
    return (
        jnp.where(front, first, pltpu.roll(second, 64, 1)),
        jnp.where(front, pltpu.roll(first, 64, 1), second),
    )


def lanes_product(even, odd, table):
    even_high, even_low = split(even)
    odd_high, odd_low = split(odd)
    out = dot(jnp.concatenate([even_high, even_low, odd_high, odd_low], axis=0), table)
    return out[:128] + out[128:256], out[256:384] + out[384:]


def rows_product(table, values):
    high, low = split(values)
    return dot(table, high) + dot(table, low)


def offsets_of(levels_ref, grid):
    return [levels_ref[grid, axis] - LOWEST[axis] for axis in range(4)]


def cover_of(offsets, b, c, d):
    _, second, third, fourth = offsets
    covered = (1 - b + b * second) * (1 - c + c * third) * (1 - d + d * fourth)
    return covered, covered * ((b * (1 + third) + c) * (1 + fourth) + d)


def own_grid():
    return lax.axis_index("half") * 8 + lax.axis_index("grid")


def forward_kernel(levels_ref, x_ref, lane_ref, row_ref, send_ref, held):
    offsets = offsets_of(levels_ref, own_grid())
    _, b_high, c_high, d_high = offsets
    count = 4 + 4 * c_high
    lane = lane_ref[d_high]
    row = row_ref[b_high]

    def step(i, _):
        t0, t1, t2, t3 = [
            x_ref[:, pl.ds(pl.multiple_of((i + j * count) * 128, 128), 128)] for j in range(4)
        ]
        even01, odd01 = swap_halves(t0, t1)
        even23, odd23 = swap_halves(t2, t3)
        even, odd = lanes_product(
            jnp.concatenate([even01, even23], axis=1),
            jnp.concatenate([odd01, odd23], axis=1),
            lane,
        )
        held[jnp.where(c_high == 1, i, 2 * i)] = even
        held[jnp.where(c_high == 1, 8 + i, 2 * i + 1)] = odd
        return 0

    lax.fori_loop(0, count, step, 0)

    @pl.when(c_high == 1)
    def _():
        for m in range(8):
            after = held[m + 1] if m < 7 else roll_lanes(held[0])
            held[8 + m] = held[8 + m] - 0.5 * (held[m] + after)

    def rows(i, _):
        out = rows_product(row, held[i])
        c = i // 8
        m = i % 8
        for b in range(2):
            for d in range(2):
                covered, slot = cover_of(offsets, b, c, d)

                @pl.when(covered == 1)
                def _():
                    for half in range(2):
                        start = b * 64 + half * 32
                        send_ref[half * 8 + m, slot] = out[
                            start : start + 32, d * 128 : d * 128 + 128
                        ]

        return 0

    lax.fori_loop(0, 8 + 8 * c_high, rows, 0)


def backward_kernel(levels_ref, recv_ref, lane_ref, row_ref, out_ref, held):
    offsets = offsets_of(levels_ref, own_grid())
    first, b_high, c_high, d_high = offsets
    count = 4 + 4 * c_high
    inside = lax.axis_index("dom") < lax.shift_left(8, first)

    @pl.when(jnp.logical_not(inside))
    def _():
        out_ref[...] = jnp.zeros_like(out_ref)

    @pl.when(inside)
    def _():
        lane = lane_ref[d_high]
        row = row_ref[b_high]

        def rows(i, _):
            c = i // 8
            m = i % 8
            columns = []
            for d in range(2):
                parts = []
                for b in range(2):
                    covered, slot = cover_of(offsets, b, c, d)
                    for half in range(2):
                        part = recv_ref[half * 8 + m, slot]
                        parts.append(jnp.where(covered == 1, part, 0.0))
                columns.append(jnp.concatenate(parts, axis=0))
            held[i] = rows_product(row, jnp.concatenate(columns, axis=1))
            return 0

        lax.fori_loop(0, 8 + 8 * c_high, rows, 0)

        @pl.when(c_high == 1)
        def _():
            for m in range(8):
                after = held[m + 1] if m < 7 else roll_lanes(held[0])
                held[8 + m] = held[8 + m] + 0.5 * (held[m] + after)

        def step(i, _):
            even, odd = lanes_product(
                held[jnp.where(c_high == 1, i, 2 * i)],
                held[jnp.where(c_high == 1, 8 + i, 2 * i + 1)],
                lane,
            )
            tiles = swap_halves(even[:, :128], odd[:, :128]) + swap_halves(
                even[:, 128:], odd[:, 128:]
            )
            for j in range(4):
                out_ref[:, pl.ds(pl.multiple_of((i + j * count) * 128, 128), 128)] = tiles[j]
            return 0

        lax.fori_loop(0, count, step, 0)

        @pl.when(c_high == 0)
        def _():
            out_ref[:, 2048:] = jnp.zeros((128, 2048), jnp.float32)


def weigh(levels_ref, weight_ref):
    guard = 0x8888
    packed = []
    for grid in range(16):
        first, second, third, fourth = offsets_of(levels_ref, grid)
        packed.append(first + 16 * second + 256 * third + 4096 * fourth)
    rows = lax.broadcasted_iota(jnp.int32, (16, 128), 0)
    corner = lax.broadcasted_iota(jnp.int32, (16, 128), 1)
    bits = [lax.shift_right_logical(corner, place) & 1 for place in range(4)]
    raised = bits[0] + 16 * bits[1] + 256 * bits[2] + 4096 * bits[3]
    for grid in range(16):
        raised = raised + jnp.where(rows == grid, packed[grid], 0)
    count = jnp.zeros((16, 128), jnp.int32)
    for grid in range(16):
        above = ((packed[grid] + guard) - raised) & guard
        count = count + jnp.where(above == guard, 1, 0)
    parity = 1 - 2 * ((bits[0] + bits[1] + bits[2] + bits[3]) & 1)
    signed = jnp.where((count > 0) & (corner < 16), parity, 0).astype(jnp.float32)
    total = jnp.sum(signed, axis=1, keepdims=True)
    weight_ref[...] = jnp.broadcast_to(total, (16, 128))


def exchange_kernel(
    levels_ref,
    send_ref,
    out_ref,
    r1a,
    r1b,
    acca,
    accb,
    r2,
    o2,
    r3a,
    r3b,
    s2,
    weight_ref,
    slot_ref,
    coef_ref,
    pick_ref,
    send1,
    recv1,
    send2,
    recv2,
    send3,
    recv3,
    send4,
    recv4,
    own,
):
    half = lax.axis_index("half")
    me = own_grid()
    dom = lax.axis_index("dom")
    far = dom // 16
    r1 = (r1a, r1b)
    acc = (acca, accb)
    r3 = (r3a, r3b)

    for s in range(8):
        r2[s, 2] = jnp.zeros((8, 128), jnp.float32)

    barrier = pltpu.get_barrier_semaphore()

    def greet_group(k, _):
        peer = (me + k) % 16
        pl.semaphore_signal(
            barrier, inc=1, device_id={"half": peer // 8, "grid": peer % 8}, device_id_type=MESH
        )
        return 0

    def greet_dom(k, _):
        pl.semaphore_signal(
            barrier, inc=1, device_id={"dom": (dom + k) % 32}, device_id_type=MESH
        )
        return 0

    lax.fori_loop(1, 16, greet_group, 0)
    lax.fori_loop(1, 32, greet_dom, 0)
    pl.semaphore_wait(barrier, 46)

    def sized(key, act):
        for option in range(3):

            @pl.when(key == option)
            def _():
                act(8 >> option)

    def copy1(c, source, peer, count):
        return pltpu.make_async_remote_copy(
            src_ref=send_ref.at[peer, pl.ds(0, count), pl.ds(16 * c, 16)],
            dst_ref=r1[c].at[source, pl.ds(0, count)],
            send_sem=send1.at[c, peer],
            recv_sem=recv1.at[c, source],
            device_id={"half": peer // 8, "grid": peer % 8},
            device_id_type=MESH,
        )

    def start1(k, _):
        peer = (me + k) % 16
        sized(half + far, lambda count: copy1(0, me, peer, count).start())
        return 0

    lax.fori_loop(1, 16, start1, 0)

    weigh(levels_ref, weight_ref)
    near = 1 - far
    nearest = jnp.where(dom < 8, 1, 0)

    def table(i, _):
        grid = i // 8
        place = i % 8
        offsets = offsets_of(levels_ref, grid)
        first, second, third, fourth = offsets
        covered, slot = cover_of(offsets, place // 4, place // 2 % 2, place % 2)
        is_two = jnp.where(first == 2, 1, 0)
        is_one = jnp.where(first == 1, 1, 0) * near
        is_zero = jnp.where(first == 0, 1, 0) * nearest
        slot_ref[i] = slot * (is_two + is_one + is_zero)
        coef_ref[3 * i] = (covered * is_two).astype(jnp.float32)
        coef_ref[3 * i + 1] = (covered * is_one).astype(jnp.float32)
        coef_ref[3 * i + 2] = (covered * is_zero).astype(jnp.float32)
        d_at = (place % 2) * fourth
        rest = place + fourth * (place // 2 - place)
        c_at = (rest % 2) * third
        rest = rest + third * (rest // 2 - rest)
        chosen = jnp.where(rest <= second, rest * 4 + c_at * 2 + d_at, 0)
        pick_ref[i] = chosen * 6 + is_one + 2 * is_zero
        return 0

    lax.fori_loop(0, 128, table, 0)

    def next1(k, _):
        peer = (me + k) % 16

        def act(count):
            copy1(0, me, peer, count).wait_send()
            copy1(1, me, peer, count).start()

        sized(half + far, act)
        return 0

    lax.fori_loop(1, 16, next1, 0)

    def tiered(key, act):
        for option in range(3):

            @pl.when(key == option)
            def _():
                act(1 + option)

    def tiers(low, high):
        return (1 - low // 16) + jnp.where((low // 8) + (high // 4) == 0, 1, 0)

    def owner(c, e):
        return (e // 2) * 4 + 2 * c + e % 2

    def copy2(c, source, e, count):
        return pltpu.make_async_remote_copy(
            src_ref=acc[c].at[e, pl.ds(0, count)],
            dst_ref=r2.at[source, pl.ds(0, count)],
            send_sem=send2.at[c, e],
            recv_sem=recv2.at[source],
            device_id={"dom": owner(c, e)},
            device_id_type=MESH,
        )

    def copy3(c, e, peer, count):
        return pltpu.make_async_remote_copy(
            src_ref=o2.at[peer, pl.ds(0, count)],
            dst_ref=r3[c].at[pl.ds(e * 3, count)],
            send_sem=send3.at[peer],
            recv_sem=recv3.at[c, e],
            device_id={"dom": peer},
            device_id_type=MESH,
        )

    def part(ref, kind, p):
        return ref[p // 2, kind, (p % 2) * 4 : (p % 2) * 4 + 4, :]

    def put(ref, kind, p, value):
        ref[p // 2, kind, (p % 2) * 4 : (p % 2) * 4 + 4, :] = value

    def joined(p):
        p = p % 32
        return part(r2, 0, 2 * p) + part(r2, 1, p)

    def coarse(q):
        q = q % 16
        return joined(2 * q) + part(r2, 2, q)

    def lift():
        for q in range(16):
            here = coarse(q)
            after = coarse(q + 1)
            middle = joined(2 * q + 1) - 0.5 * (joined(2 * q) + joined(2 * q + 2))
            put(o2, 2, q, here)
            put(o2, 1, 2 * q, here)
            put(o2, 1, 2 * q + 1, middle + 0.5 * (here + after))
        for s in range(32):
            here = part(o2, 1, s)
            after = part(o2, 1, (s + 1) % 32)
            fine = part(r2, 0, 2 * s + 1) - 0.5 * (
                part(r2, 0, 2 * s) + part(r2, 0, (2 * s + 2) % 64)
            )
            put(o2, 0, 2 * s, here)
            put(o2, 0, 2 * s + 1, fine + 0.5 * (here + after))

    def copy4(c, source, peer, count):
        return pltpu.make_async_remote_copy(
            src_ref=s2.at[peer, pl.ds(0, count), pl.ds(16 * c, 16)],
            dst_ref=out_ref.at[source, pl.ds(0, count), pl.ds(16 * c, 16)],
            send_sem=send4.at[c, peer],
            recv_sem=recv4.at[c, source],
            device_id={"half": peer // 8, "grid": peer % 8},
            device_id_type=MESH,
        )

    mine = dom // 2 % 2
    my_e = (dom // 4) * 2 + dom % 2

    for c in range(2):

        def wait1(k, _):
            source = (me + 16 - k) % 16
            sized(source // 8 + far, lambda count: copy1(c, source, source, count).wait_recv())
            return 0

        lax.fori_loop(1, 16, wait1, 0)

        def keep(slot, _):
            r1[c][me, slot] = send_ref[me, slot, pl.ds(16 * c, 16), :]
            return 0

        lax.fori_loop(0, 8, keep, 0)

        def add(block, _):
            for group in range(2):
                sums = [jnp.zeros((8, 128), jnp.float32) for _ in range(2)]
                for source in range(16):
                    at = source * 8 + block
                    value = r1[c][source, slot_ref[at], pl.ds(group * 8, 8), :]
                    value = value * weight_ref[pl.ds(source, 1), :]
                    for kind in range(2):
                        sums[kind] = sums[kind] + value * coef_ref[3 * at + kind]
                for kind in range(2):
                    acc[c][block * 2 + group, kind] = sums[kind]
            return 0

        lax.fori_loop(0, 8, add, 0)
        for group in range(2):
            total = jnp.zeros((8, 128), jnp.float32)
            for source in range(16):
                value = r1[c][source, 0, pl.ds(group * 8, 8), :]
                value = value * weight_ref[pl.ds(source, 1), :]
                total = total + value * coef_ref[3 * source * 8 + 2]
            acc[c][group, 2] = total

        def start2(k, _):
            e = (my_e + k) % 16
            peer = owner(c, e)

            @pl.when(peer != dom)
            def _():
                tiered(tiers(dom, peer), lambda count: copy2(c, dom, e, count).start())

            return 0

        lax.fori_loop(0, 16, start2, 0)

        @pl.when(mine == c)
        def _():
            for kind in range(2):
                r2[dom, kind] = acc[c][my_e, kind]

            @pl.when(dom // 4 == 0)
            def _():
                r2[dom, 2] = acc[c][my_e, 2]

            def wait2(k, _):
                source = (dom + 32 - k) % 32
                tiered(
                    tiers(source, dom), lambda count: copy2(c, source, my_e, count).wait_recv()
                )
                return 0

            lax.fori_loop(1, 32, wait2, 0)
            lift()

            def start3(k, _):
                peer = (dom + k) % 32
                tiered(tiers(peer, dom), lambda count: copy3(c, my_e, peer, count).start())
                return 0

            lax.fori_loop(1, 32, start3, 0)
            r3[c][my_e * 3] = o2[dom, 0]

            @pl.when(far == 0)
            def _():
                r3[c][my_e * 3 + 1] = o2[dom, 1]

            @pl.when(dom // 4 == 0)
            def _():
                r3[c][my_e * 3 + 2] = o2[dom, 2]

        def wait3(k, _):
            e = (my_e + 16 - k) % 16
            peer = owner(c, e)

            @pl.when(peer != dom)
            def _():
                tiered(tiers(dom, peer), lambda count: copy3(c, e, dom, count).wait_recv())

            return 0

        lax.fori_loop(0, 16, wait3, 0)

        def fill(peer):
            def one(slot, _):
                pick = pick_ref[peer * 8 + slot]
                for group in range(2):
                    s2[peer, slot, pl.ds(16 * c + group * 8, 8), :] = r3[c][pick + group * 3]
                return 0

            lax.fori_loop(0, 8, one, 0)

        def start4(k, _):
            peer = (me + k) % 16
            fill(peer)
            sized(peer // 8 + far, lambda count: copy4(c, me, peer, count).start())
            return 0

        lax.fori_loop(1, 16, start4, 0)
        fill(me)

    home = pltpu.make_async_copy(s2.at[me], out_ref.at[me], own)
    home.start()

    for c in range(2):

        def wait4(k, _):
            source = (me + 16 - k) % 16
            sized(half + far, lambda count: copy4(c, source, source, count).wait_recv())
            return 0

        lax.fori_loop(1, 16, wait4, 0)

    home.wait()

    def sent_group(k, _):
        peer = (me + k) % 16
        sized(half + far, lambda count: copy1(1, me, peer, count).wait_send())
        for c in range(2):
            sized(peer // 8 + far, lambda count: copy4(c, me, peer, count).wait_send())
        return 0

    lax.fori_loop(1, 16, sent_group, 0)

    for c in range(2):

        def sent2(e, _):
            peer = owner(c, e)

            @pl.when(peer != dom)
            def _():
                tiered(tiers(dom, peer), lambda count: copy2(c, dom, e, count).wait_send())

            return 0

        lax.fori_loop(0, 16, sent2, 0)

    def sent3(k, _):
        peer = (dom + k) % 32
        tiered(tiers(peer, dom), lambda count: copy3(0, my_e, peer, count).wait_send())
        return 0

    lax.fori_loop(1, 32, sent3, 0)


def exchange(levels, packed):
    dma = pltpu.SemaphoreType.DMA
    f32 = jnp.float32
    return pl.pallas_call(
        exchange_kernel,
        out_shape=jax.ShapeDtypeStruct((16, 8, 32, 128), f32),
        in_specs=[
            pl.BlockSpec(memory_space=pltpu.SMEM),
            pl.BlockSpec(memory_space=pltpu.VMEM),
        ],
        out_specs=pl.BlockSpec(memory_space=pl.ANY),
        scratch_shapes=[
            pltpu.VMEM((16, 8, 16, 128), f32),
            pltpu.VMEM((16, 8, 16, 128), f32),
            pltpu.VMEM((16, 3, 8, 128), f32),
            pltpu.VMEM((16, 3, 8, 128), f32),
            pltpu.VMEM((32, 3, 8, 128), f32),
            pltpu.VMEM((32, 3, 8, 128), f32),
            pltpu.VMEM((48, 8, 128), f32),
            pltpu.VMEM((48, 8, 128), f32),
            pltpu.VMEM((16, 8, 32, 128), f32),
            pltpu.VMEM((16, 128), f32),
            pltpu.SMEM((128,), jnp.int32),
            pltpu.SMEM((384,), f32),
            pltpu.SMEM((128,), jnp.int32),
            dma((2, 16)),
            dma((2, 16)),
            dma((2, 16)),
            dma((32,)),
            dma((32,)),
            dma((2, 16)),
            dma((2, 16)),
            dma((2, 16)),
            dma,
        ],
        compiler_params=pltpu.CompilerParams(
            collective_id=0, has_side_effects=True, vmem_limit_bytes=32 * 2**20
        ),
    )(levels, packed)


def local_call(kernel, levels, values, out_shape, lanes, rows):
    return pl.pallas_call(
        kernel,
        out_shape=jax.ShapeDtypeStruct(out_shape, jnp.float32),
        in_specs=[pl.BlockSpec(memory_space=pltpu.SMEM)]
        + [pl.BlockSpec(memory_space=pltpu.VMEM)] * 3,
        out_specs=pl.BlockSpec(memory_space=pltpu.VMEM),
        scratch_shapes=[pltpu.VMEM((16, 128, 256), jnp.float32)],
        compiler_params=pltpu.CompilerParams(vmem_limit_bytes=32 * 2**20),
    )(levels, values, lanes, rows)


def per_device(grids, levels):
    lane_forward, lane_backward = lane_tables()
    row_forward, row_backward = row_tables()
    packed = local_call(
        forward_kernel,
        levels,
        grids.reshape(128, 4096),
        (16, 8, 32, 128),
        lane_forward,
        row_forward,
    )
    received = exchange(levels, packed)
    combined = local_call(
        backward_kernel, levels, received, (128, 4096), lane_backward, row_backward
    )
    return combined.reshape(grids.shape)


def solution(mesh):
    return jax.shard_map(
        per_device,
        mesh=mesh,
        in_specs=(P(("half", "grid"), "dom", None, None), P()),
        out_specs=P(("half", "grid"), "dom", None, None),
        check_vma=False,
    )
```

time: 159 us -> 122 us (0.77)
  Pallas kernels: 149 us -> 118 us
  other arithmetic: 4.32 us -> 0 us
    pallas_call x1, Pallas kernels: 135 us -> 103 us  [exchange(): pl.pallas_call(exchange_kernel, out_shape=jax.ShapeDtypeStruct((16, 8, 32...]
where the time goes in v2:
time: 122 us
  Pallas kernels  118 us (97%)
  local copies, waits for them, and re-layouts  4.15 us (3%)
    pallas_call x1, Pallas kernels, exchange(): pl.pallas_call(exchange_kernel, out_shape=jax.ShapeDtypeStruct((16, 8, 32...  103 us
    pallas_call x2, Pallas kernels, local_call(): pl.pallas_call(kernel, out_shape=jax.ShapeDtypeStruct(out_shape, jnp.floa...  14.5 us
    unnamed x11, local copies, waits for them, and re-layouts  4.15 us

profile of v2, /device:TPU:50, one launch (start us, length us, event | category | flops | bytes accessed | tf_op | source)
XLA Modules:
  0.0 121.7 jit_solution(16528637179664573513)
XLA Ops:
  0.0 0.8 copy.9.levels_ref
  0.8 0.0 copy-start
  0.8 1.6 %copy-done = f32[1,2,64,4096]{3,2,1,0:T(8,128)S(1)} copy-done((f32[1,2,64,4096]{3,2,1,0:T(8,128)S(1)}, f32[1,2,64,4096]{3,2,1,0:T(8,128)}, u32[]{:S(2)}) %copy-start) | copy-done | bytes 2097176
  2.4 0.0 copy-start.2
  2.4 0.9 copy-done.2
  3.3 0.0 copy-start.4
  3.3 0.8 copy-done.4
  4.1 6.5 %shard_map.64.send_ref = f32[16,8,32,128]{3,2,1,0:T(8,128)S(1)} custom-call(s32[16,4]{1,0:T(8,128)S(1)} %copy.9.levels_ref, f32[128,4096]{1,0:T(8,128)S(1)} %bitcast.2, bf16[2,256,256]{2,1,0:T(8,128)(2,1)S(1)} %copy-done.2, bf16[2,128,128]{2,1,0:T(8,128)(2,1)S(1)} %copy-done.4), custom_call_target="tpu_custom_call" | custom-call | tf_op jit(solution)/shard_map/pallas_call | solution.py:640
  10.6 0.0 copy-start.1
  10.6 0.0 copy-start.3
  10.7 103.0 %shard_map.65.recv_ref = f32[16,8,32,128]{3,2,1,0:T(8,128)S(1)} custom-call(s32[16,4]{1,0:T(8,128)S(1)} %copy.9.levels_ref, f32[16,8,32,128]{3,2,1,0:T(8,128)S(1)} %shard_map.64.send_ref), custom_call_target="tpu_custom_call" | custom-call | tf_op jit(solution)/shard_map/pallas_call | solution.py:601
  113.7 0.0 copy-done.1
  113.7 0.0 copy-done.3
  113.7 8.1 %shard_map.66 = f32[128,4096]{1,0:T(8,128)} custom-call(s32[16,4]{1,0:T(8,128)S(1)} %copy.9.levels_ref, f32[16,8,32,128]{3,2,1,0:T(8,128)S(1)} %shard_map.65.recv_ref, bf16[2,256,256]{2,1,0:T(8,128)(2,1)S(1)} %copy-done.1, bf16[2,128,128]{2,1,0:T(8,128)(2,1)S(1)} %copy-done.3), custom_call_target="tpu_custom_call" | custom-call | tf_op jit(solution)/shard_map/pallas_call | solution.py:640
Async XLA Ops:
  0.8 1.6 %copy-start = (f32[1,2,64,4096]{3,2,1,0:T(8,128)S(1)}, f32[1,2,64,4096]{3,2,1,0:T(8,128)}, u32[]{:S(2)}) copy-start(f32[1,2,64,4096]{3,2,1,0:T(8,128)} %param.6) | copy-start | bytes 6291460
  2.4 0.9 copy-start.2
  3.3 0.8 copy-start.4
  10.6 103.0 %copy-start.1 = (bf16[2,256,256]{2,1,0:T(8,128)(2,1)S(1)}, bf16[2,256,256]{2,1,0:T(8,128)(2,1)}, u32[]{:S(2)}) copy-start(bf16[2,256,256]{2,1,0:T(8,128)(2,1)} %constant.9.clone.lane_ref) | copy-start | bytes 786436
  10.6 103.0 %copy-start.3 = (bf16[2,128,128]{2,1,0:T(8,128)(2,1)S(1)}, bf16[2,128,128]{2,1,0:T(8,128)(2,1)}, u32[]{:S(2)}) copy-start(bf16[2,128,128]{2,1,0:T(8,128)(2,1)} %constant.11.clone.row_ref) | copy-start | bytes 196612

commit v3 on v2

--- a/solution.py
+++ b/solution.py
@@ -1,6 +1,5 @@
 import jax
 import jax.numpy as jnp
-import numpy as np
 from jax import lax
 from jax.experimental import pallas as pl
 from jax.experimental.pallas import tpu as pltpu
@@ -14,49 +13,33 @@
 LOWEST = (LEV1 - 2, LEV2 - 1, LEV3 - 1, LEV4 - 1)
 
 
-def lift_tables():
-    down = np.zeros((2, 64, 64))
-    up = np.zeros((2, 64, 64))
-    for p in range(32):
-        down[0, p, p] = 1
-        up[0, p, p] = 1
-        after = (p + 1) % 32
-        down[1, p, 2 * p] = 1
-        down[1, 32 + p, 2 * p + 1] = 1
-        down[1, 32 + p, 2 * p] -= 0.5
-        down[1, 32 + p, 2 * after] -= 0.5
-        up[1, 2 * p, p] = 1
-        up[1, 2 * p + 1, 32 + p] = 1
-        up[1, 2 * p + 1, p] += 0.5
-        up[1, 2 * p + 1, after] += 0.5
-    return down, up
-
-
-def row_tables():
-    down, up = lift_tables()
-    forward = np.zeros((2, 128, 128))
-    backward = np.zeros((2, 128, 128))
-    for a in range(2):
-        for k in range(64):
-            row = (k // 4) * 8 + a * 4 + k % 4
-            forward[:, row, a * 64 : a * 64 + 64] = down[:, k, :]
-            backward[:, a * 64 : a * 64 + 64, row] = up[:, :, k]
-    return jnp.asarray(forward, jnp.bfloat16), jnp.asarray(backward, jnp.bfloat16)
-
-
-def lane_tables():
-    down, up = lift_tables()
-    forward = np.zeros((2, 4, 64, 2, 4, 32))
-    backward = np.zeros((2, 2, 4, 32, 4, 64))
-    for j in range(4):
-        for high in range(2):
-            rows = slice(32 * high, 32 * high + 32)
-            forward[:, j, :, high, j, :] = down[:, rows, :].transpose(0, 2, 1)
-            backward[:, high, j, :, j, :] = up[:, :, rows].transpose(0, 2, 1)
-    return (
-        jnp.asarray(forward.reshape(2, 256, 256), jnp.bfloat16),
-        jnp.asarray(backward.reshape(2, 256, 256), jnp.bfloat16),
-    )
+def down_entry(high, h, e, p):
+    low = jnp.where(p == e * (1 + high), 1.0, 0.0)
+    fine = jnp.where(p == 2 * e + 1, 1.0, 0.0)
+    fine = fine - jnp.where((p == 2 * e) | (p == ((2 * e + 2) & 63)), 0.5, 0.0)
+    return jnp.where(h == 0, low, fine * high.astype(jnp.float32))
+
+
+def up_entry(high, h, e, p):
+    middle = jnp.where((p == 2 * e + 1) | (p == ((2 * e + 63) & 63)), 0.5, 0.0)
+    low = jnp.where(p == e * (1 + high), 1.0, 0.0) + middle * high.astype(jnp.float32)
+    fine = jnp.where(p == 2 * e + 1, 1.0, 0.0) * high.astype(jnp.float32)
+    return jnp.where(h == 0, low, fine)
+
+
+def lane_table(entry, high, points_axis):
+    point = lax.broadcasted_iota(jnp.int32, (256, 256), points_axis)
+    place = lax.broadcasted_iota(jnp.int32, (256, 256), 1 - points_axis)
+    value = entry(high, place >> 7, place & 31, point & 63)
+    return jnp.where((point >> 6) == ((place >> 5) & 3), value, 0.0).astype(jnp.bfloat16)
+
+
+def row_table(entry, high, points_axis):
+    point = lax.broadcasted_iota(jnp.int32, (128, 128), points_axis)
+    place = lax.broadcasted_iota(jnp.int32, (128, 128), 1 - points_axis)
+    part = (place >> 3) * 4 + (place & 3)
+    value = entry(high, part >> 5, part & 31, point & 63)
+    return jnp.where((point >> 6) == ((place >> 2) & 1), value, 0.0).astype(jnp.bfloat16)
 
 
 def split(values):
@@ -96,7 +79,7 @@
 
 
 def offsets_of(levels_ref, grid):
-    return [levels_ref[grid, axis] - LOWEST[axis] for axis in range(4)]
+    return [levels_ref[axis, grid] - LOWEST[axis] for axis in range(4)]
 
 
 def cover_of(offsets, b, c, d):
@@ -109,40 +92,26 @@
     return lax.axis_index("half") * 8 + lax.axis_index("grid")
 
 
-def forward_kernel(levels_ref, x_ref, lane_ref, row_ref, send_ref, held):
+def forward_kernel(levels_ref, x_ref, send_ref, held):
     offsets = offsets_of(levels_ref, own_grid())
     _, b_high, c_high, d_high = offsets
-    count = 4 + 4 * c_high
-    lane = lane_ref[d_high]
-    row = row_ref[b_high]
-
-    def step(i, _):
-        t0, t1, t2, t3 = [
-            x_ref[:, pl.ds(pl.multiple_of((i + j * count) * 128, 128), 128)] for j in range(4)
-        ]
-        even01, odd01 = swap_halves(t0, t1)
-        even23, odd23 = swap_halves(t2, t3)
-        even, odd = lanes_product(
+    lane = lane_table(down_entry, d_high, 0)
+    row = row_table(down_entry, b_high, 1)
+
+    def tile(t):
+        return x_ref[:, t * 128 : t * 128 + 128]
+
+    def parts(i, count):
+        even01, odd01 = swap_halves(tile(i), tile(i + count))
+        even23, odd23 = swap_halves(tile(i + 2 * count), tile(i + 3 * count))
+        return lanes_product(
             jnp.concatenate([even01, even23], axis=1),
             jnp.concatenate([odd01, odd23], axis=1),
             lane,
         )
-        held[jnp.where(c_high == 1, i, 2 * i)] = even
-        held[jnp.where(c_high == 1, 8 + i, 2 * i + 1)] = odd
-        return 0
-
-    lax.fori_loop(0, count, step, 0)
-
-    @pl.when(c_high == 1)
-    def _():
-        for m in range(8):
-            after = held[m + 1] if m < 7 else roll_lanes(held[0])
-            held[8 + m] = held[8 + m] - 0.5 * (held[m] + after)
-
-    def rows(i, _):
-        out = rows_product(row, held[i])
-        c = i // 8
-        m = i % 8
+
+    def rows(c, m):
+        out = rows_product(row, held[c * 8 + m])
         for b in range(2):
             for d in range(2):
                 covered, slot = cover_of(offsets, b, c, d)
@@ -155,15 +124,28 @@
                             start : start + 32, d * 128 : d * 128 + 128
                         ]
 
-        return 0
-
-    lax.fori_loop(0, 8 + 8 * c_high, rows, 0)
-
-
-def backward_kernel(levels_ref, recv_ref, lane_ref, row_ref, out_ref, held):
+    @pl.when(c_high == 0)
+    def _():
+        for i in range(4):
+            held[2 * i], held[2 * i + 1] = parts(i, 4)
+
+    @pl.when(c_high == 1)
+    def _():
+        for i in range(8):
+            held[i], held[8 + i] = parts(i, 8)
+        for m in range(8):
+            after = held[m + 1] if m < 7 else roll_lanes(held[0])
+            held[8 + m] = held[8 + m] - 0.5 * (held[m] + after)
+        for m in range(8):
+            rows(1, m)
+
+    for m in range(8):
+        rows(0, m)
+
+
+def backward_kernel(levels_ref, recv_ref, out_ref, held):
     offsets = offsets_of(levels_ref, own_grid())
     first, b_high, c_high, d_high = offsets
-    count = 4 + 4 * c_high
     inside = lax.axis_index("dom") < lax.shift_left(8, first)
 
     @pl.when(jnp.logical_not(inside))
@@ -172,12 +154,10 @@
 
     @pl.when(inside)
     def _():
-        lane = lane_ref[d_high]
-        row = row_ref[b_high]
-
-        def rows(i, _):
-            c = i // 8
-            m = i % 8
+        lane = lane_table(up_entry, d_high, 1)
+        row = row_table(up_entry, b_high, 0)
+
+        def rows(c, m):
             columns = []
             for d in range(2):
                 parts = []
@@ -187,34 +167,32 @@
                         part = recv_ref[half * 8 + m, slot]
                         parts.append(jnp.where(covered == 1, part, 0.0))
                 columns.append(jnp.concatenate(parts, axis=0))
-            held[i] = rows_product(row, jnp.concatenate(columns, axis=1))
-            return 0
-
-        lax.fori_loop(0, 8 + 8 * c_high, rows, 0)
-
-        @pl.when(c_high == 1)
-        def _():
-            for m in range(8):
-                after = held[m + 1] if m < 7 else roll_lanes(held[0])
-                held[8 + m] = held[8 + m] + 0.5 * (held[m] + after)
-
-        def step(i, _):
-            even, odd = lanes_product(
-                held[jnp.where(c_high == 1, i, 2 * i)],
-                held[jnp.where(c_high == 1, 8 + i, 2 * i + 1)],
-                lane,
-            )
+            held[c * 8 + m] = rows_product(row, jnp.concatenate(columns, axis=1))
+
+        def step(i, count, even, odd):
+            even, odd = lanes_product(even, odd, lane)
             tiles = swap_halves(even[:, :128], odd[:, :128]) + swap_halves(
                 even[:, 128:], odd[:, 128:]
             )
             for j in range(4):
-                out_ref[:, pl.ds(pl.multiple_of((i + j * count) * 128, 128), 128)] = tiles[j]
-            return 0
-
-        lax.fori_loop(0, count, step, 0)
+                t = i + j * count
+                out_ref[:, t * 128 : t * 128 + 128] = tiles[j]
+
+        for m in range(8):
+            rows(0, m)
+
+        @pl.when(c_high == 1)
+        def _():
+            for m in range(8):
+                rows(1, m)
+            for m in range(8):
+                after = held[m + 1] if m < 7 else roll_lanes(held[0])
+                step(m, 8, held[m], held[8 + m] + 0.5 * (held[m] + after))
 
         @pl.when(c_high == 0)
         def _():
+            for i in range(4):
+                step(i, 4, held[2 * i], held[2 * i + 1])
             out_ref[:, 2048:] = jnp.zeros((128, 2048), jnp.float32)
 
 
@@ -266,6 +244,12 @@
     send4,
     recv4,
     own,
+    ra,
+    rb,
+    sendr,
+    recvr,
+    sendf,
+    recvf,
 ):
     half = lax.axis_index("half")
     me = own_grid()
@@ -274,6 +258,8 @@
     r1 = (r1a, r1b)
     acc = (acca, accb)
     r3 = (r3a, r3b)
+    relayed = (ra, rb)
+    line = me % 8
 
     for s in range(8):
         r2[s, 2] = jnp.zeros((8, 128), jnp.float32)
@@ -314,9 +300,67 @@
             device_id_type=MESH,
         )
 
+    def shared(source_half, across, act):
+        key = source_half + far
+
+        @pl.when((key == 0) & across)
+        def _():
+            act(8)
+
+        @pl.when((key == 0) & jnp.logical_not(across))
+        def _():
+            act(6)
+
+        @pl.when(key == 1)
+        def _():
+            act(4)
+
+        @pl.when(key == 2)
+        def _():
+            act(2)
+
+    def relay(c):
+        return pltpu.make_async_remote_copy(
+            src_ref=send_ref.at[:, pl.ds(6, 2), pl.ds(16 * c, 16)],
+            dst_ref=relayed[c],
+            send_sem=sendr.at[c],
+            recv_sem=recvr.at[c],
+            device_id={"half": 1 - half},
+            device_id_type=MESH,
+        )
+
+    def forward(c, source, peer):
+        return pltpu.make_async_remote_copy(
+            src_ref=relayed[c].at[peer],
+            dst_ref=r1[c].at[source, pl.ds(6, 2)],
+            send_sem=sendf.at[c, peer],
+            recv_sem=recvf.at[c, source],
+            device_id={"half": peer // 8, "grid": peer % 8},
+            device_id_type=MESH,
+        )
+
+    gives = half + far == 0
+    takes = (half == 1) & (far == 0)
+
+    def pass_on(c):
+        @pl.when(takes)
+        def _():
+            relay(c).wait_recv()
+
+            def one(k, _):
+                for side in range(2):
+                    forward(c, line, side * 8 + (line + k) % 8).start()
+                return 0
+
+            lax.fori_loop(1, 8, one, 0)
+
+    @pl.when(gives)
+    def _():
+        relay(0).start()
+
     def start1(k, _):
         peer = (me + k) % 16
-        sized(half + far, lambda count: copy1(0, me, peer, count).start())
+        shared(half, peer % 8 == line, lambda count: copy1(0, me, peer, count).start())
         return 0
 
     lax.fori_loop(1, 16, start1, 0)
@@ -348,6 +392,13 @@
 
     lax.fori_loop(0, 128, table, 0)
 
+    @pl.when(gives)
+    def _():
+        relay(0).wait_send()
+        relay(1).start()
+
+    pass_on(0)
+
     def next1(k, _):
         peer = (me + k) % 16
 
@@ -355,10 +406,11 @@
             copy1(0, me, peer, count).wait_send()
             copy1(1, me, peer, count).start()
 
-        sized(half + far, act)
+        shared(half, peer % 8 == line, act)
         return 0
 
     lax.fori_loop(1, 16, next1, 0)
+    pass_on(1)
 
     def tiered(key, act):
         for option in range(3):
@@ -437,15 +489,21 @@
     mine = dom // 2 % 2
     my_e = (dom // 4) * 2 + dom % 2
 
-    for c in range(2):
-
+    def arrive(c):
         def wait1(k, _):
             source = (me + 16 - k) % 16
-            sized(source // 8 + far, lambda count: copy1(c, source, source, count).wait_recv())
+            across = source % 8 == line
+            shared(source // 8, across, lambda count: copy1(c, source, source, count).wait_recv())
+
+            @pl.when((source // 8 + far == 0) & jnp.logical_not(across))
+            def _():
+                forward(c, source % 8, source).wait_recv()
+
             return 0
 
         lax.fori_loop(1, 16, wait1, 0)
 
+    def summed(c):
         def keep(slot, _):
             r1[c][me, slot] = send_ref[me, slot, pl.ds(16 * c, 16), :]
             return 0
@@ -486,6 +544,7 @@
 
         lax.fori_loop(0, 16, start2, 0)
 
+    def owned(c):
         @pl.when(mine == c)
         def _():
             for kind in range(2):
@@ -521,6 +580,7 @@
             def _():
                 r3[c][my_e * 3 + 2] = o2[dom, 2]
 
+    def deliver(c):
         def wait3(k, _):
             e = (my_e + 16 - k) % 16
             peer = owner(c, e)
@@ -551,6 +611,15 @@
         lax.fori_loop(1, 16, start4, 0)
         fill(me)
 
+    arrive(0)
+    summed(0)
+    owned(0)
+    arrive(1)
+    deliver(0)
+    summed(1)
+    owned(1)
+    deliver(1)
+
     home = pltpu.make_async_copy(s2.at[me], out_ref.at[me], own)
     home.start()
 
@@ -567,12 +636,26 @@
 
     def sent_group(k, _):
         peer = (me + k) % 16
-        sized(half + far, lambda count: copy1(1, me, peer, count).wait_send())
+        shared(half, peer % 8 == line, lambda count: copy1(1, me, peer, count).wait_send())
         for c in range(2):
             sized(peer // 8 + far, lambda count: copy4(c, me, peer, count).wait_send())
         return 0
 
     lax.fori_loop(1, 16, sent_group, 0)
+
+    @pl.when(gives)
+    def _():
+        relay(1).wait_send()
+
+    @pl.when(takes)
+    def _():
+        def passed(k, _):
+            for c in range(2):
+                for side in range(2):
+                    forward(c, line, side * 8 + (line + k) % 8).wait_send()
+            return 0
+
+        lax.fori_loop(1, 8, passed, 0)
 
     for c in range(2):
 
@@ -629,6 +712,12 @@
             dma((2, 16)),
             dma((2, 16)),
             dma,
+            pltpu.VMEM((16, 2, 16, 128), f32),
+            pltpu.VMEM((16, 2, 16, 128), f32),
+            dma((2,)),
+            dma((2,)),
+            dma((2, 16)),
+            dma((2, 8)),
         ],
         compiler_params=pltpu.CompilerParams(
             collective_id=0, has_side_effects=True, vmem_limit_bytes=32 * 2**20
@@ -636,33 +725,25 @@
     )(levels, packed)
 
 
-def local_call(kernel, levels, values, out_shape, lanes, rows):
+def local_call(kernel, levels, values, out_shape):
     return pl.pallas_call(
         kernel,
         out_shape=jax.ShapeDtypeStruct(out_shape, jnp.float32),
-        in_specs=[pl.BlockSpec(memory_space=pltpu.SMEM)]
-        + [pl.BlockSpec(memory_space=pltpu.VMEM)] * 3,
+        in_specs=[
+            pl.BlockSpec(memory_space=pltpu.SMEM),
+            pl.BlockSpec(memory_space=pltpu.VMEM),
+        ],
         out_specs=pl.BlockSpec(memory_space=pltpu.VMEM),
         scratch_shapes=[pltpu.VMEM((16, 128, 256), jnp.float32)],
         compiler_params=pltpu.CompilerParams(vmem_limit_bytes=32 * 2**20),
-    )(levels, values, lanes, rows)
+    )(levels, values)
 
 
 def per_device(grids, levels):
-    lane_forward, lane_backward = lane_tables()
-    row_forward, row_backward = row_tables()
-    packed = local_call(
-        forward_kernel,
-        levels,
-        grids.reshape(128, 4096),
-        (16, 8, 32, 128),
-        lane_forward,
-        row_forward,
-    )
-    received = exchange(levels, packed)
-    combined = local_call(
-        backward_kernel, levels, received, (128, 4096), lane_backward, row_backward
-    )
+    turned = levels.T
+    packed = local_call(forward_kernel, turned, grids.reshape(128, 4096), (16, 8, 32, 128))
+    received = exchange(turned, packed)
+    combined = local_call(backward_kernel, turned, received, (128, 4096))
     return combined.reshape(grids.shape)
 
 

time: 122 us -> 117 us (0.959)
  the two profiles are of different devices: /device:TPU:50 before, /device:TPU:49 now
where the time goes in v3:
time: 117 us
  Pallas kernels  115 us (98%)
  local copies, waits for them, and re-layouts  2.27 us (2%)
    pallas_call x1, Pallas kernels, exchange(): pl.pallas_call(exchange_kernel, out_shape=jax.ShapeDtypeStruct((16, 8, 32...  109 us
    pallas_call x2, Pallas kernels, local_call(): pl.pallas_call(kernel, out_shape=jax.ShapeDtypeStruct(out_shape, jnp.floa...  6.05 us

profile of v3, /device:TPU:49, one launch (start us, length us, event | category | flops | bytes accessed | tf_op | source)
XLA Modules:
  0.0 117.2 jit_solution(14076670784188654802)
XLA Ops:
  0.0 0.0 copy-start
  0.0 1.6 %copy-done = f32[1,2,64,4096]{3,2,1,0:T(8,128)S(1)} copy-done((f32[1,2,64,4096]{3,2,1,0:T(8,128)S(1)}, f32[1,2,64,4096]{3,2,1,0:T(8,128)}, u32[]{:S(2)}) %copy-start) | copy-done | bytes 2097176
  1.6 0.0 copy-start.1
  1.6 0.7 copy-done.1
  2.3 2.9 %shard_map.28.send_ref = f32[16,8,32,128]{3,2,1,0:T(8,128)S(1)} custom-call(s32[4,16]{1,0:T(4,128)S(1)} %bitcast.4, f32[128,4096]{1,0:T(8,128)S(1)} %bitcast.3), custom_call_target="tpu_custom_call" | custom-call | tf_op jit(solution)/shard_map/pallas_call | solution.py:729
  5.2 108.8 %shard_map.29.recv_ref = f32[16,8,32,128]{3,2,1,0:T(8,128)S(1)} custom-call(s32[4,16]{1,0:T(4,128)S(1)} %bitcast.5, f32[16,8,32,128]{3,2,1,0:T(8,128)S(1)} %shard_map.28.send_ref), custom_call_target="tpu_custom_call" | custom-call | tf_op jit(solution)/shard_map/pallas_call | solution.py:684
  114.0 3.1 %shard_map.30 = f32[128,4096]{1,0:T(8,128)} custom-call(s32[4,16]{1,0:T(4,128)S(1)} %bitcast.6, f32[16,8,32,128]{3,2,1,0:T(8,128)S(1)} %shard_map.29.recv_ref), custom_call_target="tpu_custom_call" | custom-call | tf_op jit(solution)/shard_map/pallas_call | solution.py:729
Async XLA Ops:
  0.0 1.6 %copy-start = (f32[1,2,64,4096]{3,2,1,0:T(8,128)S(1)}, f32[1,2,64,4096]{3,2,1,0:T(8,128)}, u32[]{:S(2)}) copy-start(f32[1,2,64,4096]{3,2,1,0:T(8,128)} %param.2) | copy-start | bytes 6291460
  1.6 0.7 copy-start.1

commit v4 on v3

--- a/solution.py
+++ b/solution.py
@@ -218,48 +218,43 @@
     weight_ref[...] = jnp.broadcast_to(total, (16, 128))
 
 
-def exchange_kernel(
-    levels_ref,
-    send_ref,
-    out_ref,
-    r1a,
-    r1b,
-    acca,
-    accb,
-    r2,
-    o2,
-    r3a,
-    r3b,
-    s2,
-    weight_ref,
-    slot_ref,
-    coef_ref,
-    pick_ref,
-    send1,
-    recv1,
-    send2,
-    recv2,
-    send3,
-    recv3,
-    send4,
-    recv4,
-    own,
-    ra,
-    rb,
-    sendr,
-    recvr,
-    sendf,
-    recvf,
-):
+def exchange_kernel(levels_ref, send_ref, out_ref, *scratch):
+    (
+        r1,
+        acc,
+        r3,
+        first_relay,
+        second_relay,
+        r2,
+        o2,
+        s2,
+        weight_ref,
+        slot_ref,
+        coef_ref,
+        pick_ref,
+        send1,
+        recv1,
+        send2,
+        recv2,
+        send3,
+        recv3,
+        send4,
+        recv4,
+        sendr,
+        recvr,
+        sendf,
+        recvf,
+        own,
+    ) = [scratch[4 * i : 4 * i + 4] for i in range(5)] + list(scratch[20:])
     half = lax.axis_index("half")
-    me = own_grid()
+    line = lax.axis_index("grid")
+    me = half * 8 + line
     dom = lax.axis_index("dom")
     far = dom // 16
-    r1 = (r1a, r1b)
-    acc = (acca, accb)
-    r3 = (r3a, r3b)
-    relayed = (ra, rb)
-    line = me % 8
+    twin = dom + 2 - 4 * (dom // 2 % 2)
+    mine = dom % 4
+    my_e = dom // 4
+    relayed = (first_relay, second_relay)
 
     for s in range(8):
         r2[s, 2] = jnp.zeros((8, 128), jnp.float32)
@@ -279,9 +274,22 @@
         )
         return 0
 
+    def greet_twin(k, _):
+        pl.semaphore_signal(
+            barrier,
+            inc=1,
+            device_id={"half": 1 - half, "grid": k, "dom": twin},
+            device_id_type=MESH,
+        )
+        return 0
+
     lax.fori_loop(1, 16, greet_group, 0)
     lax.fori_loop(1, 32, greet_dom, 0)
-    pl.semaphore_wait(barrier, 46)
+    lax.fori_loop(0, 8, greet_twin, 0)
+    pl.semaphore_wait(barrier, 54)
+
+    def rows(c):
+        return pl.ds(8 * c, 8)
 
     def sized(key, act):
         for option in range(3):
@@ -292,7 +300,7 @@
 
     def copy1(c, source, peer, count):
         return pltpu.make_async_remote_copy(
-            src_ref=send_ref.at[peer, pl.ds(0, count), pl.ds(16 * c, 16)],
+            src_ref=send_ref.at[peer, pl.ds(0, count), rows(c)],
             dst_ref=r1[c].at[source, pl.ds(0, count)],
             send_sem=send1.at[c, peer],
             recv_sem=recv1.at[c, source],
@@ -319,23 +327,25 @@
         def _():
             act(2)
 
-    def relay(c):
+    def relay(way, c):
+        target = {"half": 1 - half} if way == 0 else {"half": 1 - half, "dom": twin}
         return pltpu.make_async_remote_copy(
-            src_ref=send_ref.at[:, pl.ds(6, 2), pl.ds(16 * c, 16)],
-            dst_ref=relayed[c],
-            send_sem=sendr.at[c],
-            recv_sem=recvr.at[c],
-            device_id={"half": 1 - half},
+            src_ref=send_ref.at[pl.ds(8 - 8 * way, 8), pl.ds(6, 2), rows(c)],
+            dst_ref=relayed[way][c],
+            send_sem=sendr.at[way, c],
+            recv_sem=recvr.at[way, c],
+            device_id=target,
             device_id_type=MESH,
         )
 
-    def forward(c, source, peer):
+    def forward(way, c, source, to):
+        target = {"grid": to} if way == 0 else {"half": 1 - half, "grid": to, "dom": twin}
         return pltpu.make_async_remote_copy(
-            src_ref=relayed[c].at[peer],
+            src_ref=relayed[way][c].at[to],
             dst_ref=r1[c].at[source, pl.ds(6, 2)],
-            send_sem=sendf.at[c, peer],
+            send_sem=sendf.at[way, c, to],
             recv_sem=recvf.at[c, source],
-            device_id={"half": peer // 8, "grid": peer % 8},
+            device_id=target,
             device_id_type=MESH,
         )
 
@@ -345,25 +355,31 @@
     def pass_on(c):
         @pl.when(takes)
         def _():
-            relay(c).wait_recv()
-
-            def one(k, _):
-                for side in range(2):
-                    forward(c, line, side * 8 + (line + k) % 8).start()
-                return 0
-
-            lax.fori_loop(1, 8, one, 0)
+            for way in range(2):
+                relay(way, c).wait_recv()
+
+                def one(k, _):
+                    forward(way, c, line, (line + k) % 8).start()
+                    return 0
+
+                lax.fori_loop(1, 8, one, 0)
+
+    def start1(c):
+        def one(k, _):
+            peer = (me + k) % 16
+            shared(half, peer % 8 == line, lambda count: copy1(c, me, peer, count).start())
+            return 0
+
+        lax.fori_loop(1, 16, one, 0)
 
     @pl.when(gives)
     def _():
-        relay(0).start()
-
-    def start1(k, _):
-        peer = (me + k) % 16
-        shared(half, peer % 8 == line, lambda count: copy1(0, me, peer, count).start())
-        return 0
-
-    lax.fori_loop(1, 16, start1, 0)
+        for c in range(4):
+            for way in range(2):
+                relay(way, c).start()
+
+    start1(0)
+    start1(1)
 
     weigh(levels_ref, weight_ref)
     near = 1 - far
@@ -387,30 +403,10 @@
         c_at = (rest % 2) * third
         rest = rest + third * (rest // 2 - rest)
         chosen = jnp.where(rest <= second, rest * 4 + c_at * 2 + d_at, 0)
-        pick_ref[i] = chosen * 6 + is_one + 2 * is_zero
+        pick_ref[i] = chosen * 3 + is_one + 2 * is_zero
         return 0
 
     lax.fori_loop(0, 128, table, 0)
-
-    @pl.when(gives)
-    def _():
-        relay(0).wait_send()
-        relay(1).start()
-
-    pass_on(0)
-
-    def next1(k, _):
-        peer = (me + k) % 16
-
-        def act(count):
-            copy1(0, me, peer, count).wait_send()
-            copy1(1, me, peer, count).start()
-
-        shared(half, peer % 8 == line, act)
-        return 0
-
-    lax.fori_loop(1, 16, next1, 0)
-    pass_on(1)
 
     def tiered(key, act):
         for option in range(3):
@@ -423,7 +419,7 @@
         return (1 - low // 16) + jnp.where((low // 8) + (high // 4) == 0, 1, 0)
 
     def owner(c, e):
-        return (e // 2) * 4 + 2 * c + e % 2
+        return 4 * e + c
 
     def copy2(c, source, e, count):
         return pltpu.make_async_remote_copy(
@@ -442,6 +438,16 @@
             send_sem=send3.at[peer],
             recv_sem=recv3.at[c, e],
             device_id={"dom": peer},
+            device_id_type=MESH,
+        )
+
+    def copy4(c, source, peer, count):
+        return pltpu.make_async_remote_copy(
+            src_ref=s2.at[peer, pl.ds(0, count), rows(c)],
+            dst_ref=out_ref.at[source, pl.ds(0, count), rows(c)],
+            send_sem=send4.at[c, peer],
+            recv_sem=recv4.at[c, source],
+            device_id={"half": peer // 8, "grid": peer % 8},
             device_id_type=MESH,
         )
 
@@ -476,19 +482,6 @@
             put(o2, 0, 2 * s, here)
             put(o2, 0, 2 * s + 1, fine + 0.5 * (here + after))
 
-    def copy4(c, source, peer, count):
-        return pltpu.make_async_remote_copy(
-            src_ref=s2.at[peer, pl.ds(0, count), pl.ds(16 * c, 16)],
-            dst_ref=out_ref.at[source, pl.ds(0, count), pl.ds(16 * c, 16)],
-            send_sem=send4.at[c, peer],
-            recv_sem=recv4.at[c, source],
-            device_id={"half": peer // 8, "grid": peer % 8},
-            device_id_type=MESH,
-        )
-
-    mine = dom // 2 % 2
-    my_e = (dom // 4) * 2 + dom % 2
-
     def arrive(c):
         def wait1(k, _):
             source = (me + 16 - k) % 16
@@ -497,7 +490,7 @@
 
             @pl.when((source // 8 + far == 0) & jnp.logical_not(across))
             def _():
-                forward(c, source % 8, source).wait_recv()
+                forward(0, c, source % 8, source % 8).wait_recv()
 
             return 0
 
@@ -505,35 +498,31 @@
 
     def summed(c):
         def keep(slot, _):
-            r1[c][me, slot] = send_ref[me, slot, pl.ds(16 * c, 16), :]
+            r1[c][me, slot] = send_ref[me, slot, rows(c), :]
             return 0
 
         lax.fori_loop(0, 8, keep, 0)
 
         def add(block, _):
-            for group in range(2):
-                sums = [jnp.zeros((8, 128), jnp.float32) for _ in range(2)]
-                for source in range(16):
-                    at = source * 8 + block
-                    value = r1[c][source, slot_ref[at], pl.ds(group * 8, 8), :]
-                    value = value * weight_ref[pl.ds(source, 1), :]
-                    for kind in range(2):
-                        sums[kind] = sums[kind] + value * coef_ref[3 * at + kind]
+            sums = [jnp.zeros((8, 128), jnp.float32) for _ in range(2)]
+            for source in range(16):
+                at = source * 8 + block
+                value = r1[c][source, slot_ref[at]] * weight_ref[pl.ds(source, 1), :]
                 for kind in range(2):
-                    acc[c][block * 2 + group, kind] = sums[kind]
+                    sums[kind] = sums[kind] + value * coef_ref[3 * at + kind]
+            for kind in range(2):
+                acc[c][block, kind] = sums[kind]
             return 0
 
         lax.fori_loop(0, 8, add, 0)
-        for group in range(2):
-            total = jnp.zeros((8, 128), jnp.float32)
-            for source in range(16):
-                value = r1[c][source, 0, pl.ds(group * 8, 8), :]
-                value = value * weight_ref[pl.ds(source, 1), :]
-                total = total + value * coef_ref[3 * source * 8 + 2]
-            acc[c][group, 2] = total
+        total = jnp.zeros((8, 128), jnp.float32)
+        for source in range(16):
+            value = r1[c][source, 0] * weight_ref[pl.ds(source, 1), :]
+            total = total + value * coef_ref[3 * source * 8 + 2]
+        acc[c][0, 2] = total
 
         def start2(k, _):
-            e = (my_e + k) % 16
+            e = (my_e + k) % 8
             peer = owner(c, e)
 
             @pl.when(peer != dom)
@@ -542,7 +531,7 @@
 
             return 0
 
-        lax.fori_loop(0, 16, start2, 0)
+        lax.fori_loop(0, 8, start2, 0)
 
     def owned(c):
         @pl.when(mine == c)
@@ -550,7 +539,7 @@
             for kind in range(2):
                 r2[dom, kind] = acc[c][my_e, kind]
 
-            @pl.when(dom // 4 == 0)
+            @pl.when(my_e == 0)
             def _():
                 r2[dom, 2] = acc[c][my_e, 2]
 
@@ -576,13 +565,13 @@
             def _():
                 r3[c][my_e * 3 + 1] = o2[dom, 1]
 
-            @pl.when(dom // 4 == 0)
+            @pl.when(my_e == 0)
             def _():
                 r3[c][my_e * 3 + 2] = o2[dom, 2]
 
     def deliver(c):
         def wait3(k, _):
-            e = (my_e + 16 - k) % 16
+            e = (my_e + 8 - k) % 8
             peer = owner(c, e)
 
             @pl.when(peer != dom)
@@ -591,16 +580,11 @@
 
             return 0
 
-        lax.fori_loop(0, 16, wait3, 0)
+        lax.fori_loop(0, 8, wait3, 0)
 
         def fill(peer):
-            def one(slot, _):
-                pick = pick_ref[peer * 8 + slot]
-                for group in range(2):
-                    s2[peer, slot, pl.ds(16 * c + group * 8, 8), :] = r3[c][pick + group * 3]
-                return 0
-
-            lax.fori_loop(0, 8, one, 0)
+            for slot in range(8):
+                s2[peer, slot, rows(c), :] = r3[c][pick_ref[peer * 8 + slot]]
 
         def start4(k, _):
             peer = (me + k) % 16
@@ -611,19 +595,33 @@
         lax.fori_loop(1, 16, start4, 0)
         fill(me)
 
+    pass_on(0)
+    pass_on(1)
     arrive(0)
+    start1(2)
     summed(0)
+    pass_on(2)
     owned(0)
     arrive(1)
+    start1(3)
+    summed(1)
+    pass_on(3)
+    owned(1)
+    arrive(2)
+    summed(2)
+    owned(2)
     deliver(0)
-    summed(1)
-    owned(1)
+    arrive(3)
+    summed(3)
     deliver(1)
+    owned(3)
+    deliver(2)
+    deliver(3)
 
     home = pltpu.make_async_copy(s2.at[me], out_ref.at[me], own)
     home.start()
 
-    for c in range(2):
+    for c in range(4):
 
         def wait4(k, _):
             source = (me + 16 - k) % 16
@@ -636,8 +634,8 @@
 
     def sent_group(k, _):
         peer = (me + k) % 16
-        shared(half, peer % 8 == line, lambda count: copy1(1, me, peer, count).wait_send())
-        for c in range(2):
+        for c in range(4):
+            shared(half, peer % 8 == line, lambda count: copy1(c, me, peer, count).wait_send())
             sized(peer // 8 + far, lambda count: copy4(c, me, peer, count).wait_send())
         return 0
 
@@ -645,19 +643,21 @@
 
     @pl.when(gives)
     def _():
-        relay(1).wait_send()
+        for c in range(4):
+            for way in range(2):
+                relay(way, c).wait_send()
 
     @pl.when(takes)
     def _():
         def passed(k, _):
-            for c in range(2):
-                for side in range(2):
-                    forward(c, line, side * 8 + (line + k) % 8).wait_send()
+            for c in range(4):
+                for way in range(2):
+                    forward(way, c, line, (line + k) % 8).wait_send()
             return 0
 
         lax.fori_loop(1, 8, passed, 0)
 
-    for c in range(2):
+    for c in range(4):
 
         def sent2(e, _):
             peer = owner(c, e)
@@ -668,7 +668,7 @@
 
             return 0
 
-        lax.fori_loop(0, 16, sent2, 0)
+        lax.fori_loop(0, 8, sent2, 0)
 
     def sent3(k, _):
         peer = (dom + k) % 32
@@ -689,35 +689,31 @@
             pl.BlockSpec(memory_space=pltpu.VMEM),
         ],
         out_specs=pl.BlockSpec(memory_space=pl.ANY),
-        scratch_shapes=[
-            pltpu.VMEM((16, 8, 16, 128), f32),
-            pltpu.VMEM((16, 8, 16, 128), f32),
-            pltpu.VMEM((16, 3, 8, 128), f32),
-            pltpu.VMEM((16, 3, 8, 128), f32),
+        scratch_shapes=[pltpu.VMEM((16, 8, 8, 128), f32)] * 4
+        + [pltpu.VMEM((8, 3, 8, 128), f32)] * 4
+        + [pltpu.VMEM((24, 8, 128), f32)] * 4
+        + [pltpu.VMEM((8, 2, 8, 128), f32)] * 8
+        + [
             pltpu.VMEM((32, 3, 8, 128), f32),
             pltpu.VMEM((32, 3, 8, 128), f32),
-            pltpu.VMEM((48, 8, 128), f32),
-            pltpu.VMEM((48, 8, 128), f32),
             pltpu.VMEM((16, 8, 32, 128), f32),
             pltpu.VMEM((16, 128), f32),
             pltpu.SMEM((128,), jnp.int32),
             pltpu.SMEM((384,), f32),
             pltpu.SMEM((128,), jnp.int32),
-            dma((2, 16)),
-            dma((2, 16)),
-            dma((2, 16)),
+            dma((4, 16)),
+            dma((4, 16)),
+            dma((4, 8)),
             dma((32,)),
             dma((32,)),
-            dma((2, 16)),
-            dma((2, 16)),
-            dma((2, 16)),
+            dma((4, 8)),
+            dma((4, 16)),
+            dma((4, 16)),
+            dma((2, 4)),
+            dma((2, 4)),
+            dma((2, 4, 8)),
+            dma((4, 8)),
             dma,
-            pltpu.VMEM((16, 2, 16, 128), f32),
-            pltpu.VMEM((16, 2, 16, 128), f32),
-            dma((2,)),
-            dma((2,)),
-            dma((2, 16)),
-            dma((2, 8)),
         ],
         compiler_params=pltpu.CompilerParams(
             collective_id=0, has_side_effects=True, vmem_limit_bytes=32 * 2**20

time: 117 us -> 106 us (0.906)
  the two profiles are of different devices: /device:TPU:49 before, /device:TPU:1 now
where the time goes in v4:
time: 106 us; the launch traced here: 105 us
  Pallas kernels  102 us (96%)
  local copies, waits for them, and re-layouts  2.27 us (2%)
    pallas_call x1, Pallas kernels, exchange(): pl.pallas_call(exchange_kernel, out_shape=jax.ShapeDtypeStruct((16, 8, 32...  94 us
    pallas_call x2, Pallas kernels, local_call(): pl.pallas_call(kernel, out_shape=jax.ShapeDtypeStruct(out_shape, jnp.floa...  8.38 us
    unnamed x4, local copies, waits for them, and re-layouts  2.27 us

profile of v4, /device:TPU:1, one launch (start us, length us, event | category | flops | bytes accessed | tf_op | source)
XLA Modules:
  0.0 104.6 jit_solution(13620357647678765669)
XLA Ops:
  0.0 0.0 copy-start
  0.0 1.6 %copy-done = f32[1,2,64,4096]{3,2,1,0:T(8,128)S(1)} copy-done((f32[1,2,64,4096]{3,2,1,0:T(8,128)S(1)}, f32[1,2,64,4096]{3,2,1,0:T(8,128)}, u32[]{:S(2)}) %copy-start) | copy-done | bytes 2097176
  1.6 0.0 copy-start.1
  1.6 0.7 copy-done.1
  2.3 4.7 %shard_map.28.send_ref = f32[16,8,32,128]{3,2,1,0:T(8,128)S(1)} custom-call(s32[4,16]{1,0:T(4,128)S(1)} %bitcast.4, f32[128,4096]{1,0:T(8,128)S(1)} %bitcast.3), custom_call_target="tpu_custom_call" | custom-call | tf_op jit(solution)/shard_map/pallas_call | solution.py:725
  7.0 94.0 %shard_map.29.recv_ref = f32[16,8,32,128]{3,2,1,0:T(8,128)S(1)} custom-call(s32[4,16]{1,0:T(4,128)S(1)} %bitcast.5, f32[16,8,32,128]{3,2,1,0:T(8,128)S(1)} %shard_map.28.send_ref), custom_call_target="tpu_custom_call" | custom-call | tf_op jit(solution)/shard_map/pallas_call | solution.py:684
  100.9 3.7 %shard_map.30 = f32[128,4096]{1,0:T(8,128)} custom-call(s32[4,16]{1,0:T(4,128)S(1)} %bitcast.6, f32[16,8,32,128]{3,2,1,0:T(8,128)S(1)} %shard_map.29.recv_ref), custom_call_target="tpu_custom_call" | custom-call | tf_op jit(solution)/shard_map/pallas_call | solution.py:725
Async XLA Ops:
  0.0 1.6 %copy-start = (f32[1,2,64,4096]{3,2,1,0:T(8,128)S(1)}, f32[1,2,64,4096]{3,2,1,0:T(8,128)}, u32[]{:S(2)}) copy-start(f32[1,2,64,4096]{3,2,1,0:T(8,128)} %param.2) | copy-start | bytes 6291460
  1.6 0.7 copy-start.1

commit v5 on v4

--- a/solution.py
+++ b/solution.py
@@ -92,55 +92,51 @@
     return lax.axis_index("half") * 8 + lax.axis_index("grid")
 
 
-def forward_kernel(levels_ref, x_ref, send_ref, held):
-    offsets = offsets_of(levels_ref, own_grid())
+def blocks_of(offsets, slot):
+    _, second, third, fourth = offsets
+    d_at = (slot % 2) * fourth
+    rest = slot + fourth * (slot // 2 - slot)
+    c_at = (rest % 2) * third
+    rest = rest + third * (rest // 2 - rest)
+    return jnp.where(rest <= second, rest * 4 + c_at * 2 + d_at, 0)
+
+
+def lower(offsets, x_ref, held, blocks_ref):
     _, b_high, c_high, d_high = offsets
     lane = lane_table(down_entry, d_high, 0)
     row = row_table(down_entry, b_high, 1)
-
-    def tile(t):
-        return x_ref[:, t * 128 : t * 128 + 128]
-
-    def parts(i, count):
-        even01, odd01 = swap_halves(tile(i), tile(i + count))
-        even23, odd23 = swap_halves(tile(i + 2 * count), tile(i + 3 * count))
-        return lanes_product(
+    fine = c_high == 1
+
+    def tile(i, j):
+        t = i + 8 * j
+        u = i % 4 + 4 * j
+        return jnp.where(
+            fine, x_ref[:, t * 128 : t * 128 + 128], x_ref[:, u * 128 : u * 128 + 128]
+        )
+
+    for i in range(8):
+        even01, odd01 = swap_halves(tile(i, 0), tile(i, 1))
+        even23, odd23 = swap_halves(tile(i, 2), tile(i, 3))
+        held[i], held[8 + i] = lanes_product(
             jnp.concatenate([even01, even23], axis=1),
             jnp.concatenate([odd01, odd23], axis=1),
             lane,
         )
-
-    def rows(c, m):
-        out = rows_product(row, held[c * 8 + m])
-        for b in range(2):
-            for d in range(2):
-                covered, slot = cover_of(offsets, b, c, d)
-
-                @pl.when(covered == 1)
-                def _():
+    for m in range(7, -1, -1):
+        held[16 + m] = jnp.where(fine, held[m], held[m // 2 + 8 * (m % 2)])
+    for m in range(8):
+        after = held[17 + m] if m < 7 else roll_lanes(held[16])
+        held[8 + m] = held[8 + m] - 0.5 * (held[16 + m] + after)
+    for c in range(2):
+        for m in range(8):
+            out = rows_product(row, held[16 - 8 * c + m])
+            for b in range(2):
+                for d in range(2):
                     for half in range(2):
                         start = b * 64 + half * 32
-                        send_ref[half * 8 + m, slot] = out[
+                        blocks_ref[half * 8 + m, b * 4 + c * 2 + d] = out[
                             start : start + 32, d * 128 : d * 128 + 128
                         ]
-
-    @pl.when(c_high == 0)
-    def _():
-        for i in range(4):
-            held[2 * i], held[2 * i + 1] = parts(i, 4)
-
-    @pl.when(c_high == 1)
-    def _():
-        for i in range(8):
-            held[i], held[8 + i] = parts(i, 8)
-        for m in range(8):
-            after = held[m + 1] if m < 7 else roll_lanes(held[0])
-            held[8 + m] = held[8 + m] - 0.5 * (held[m] + after)
-        for m in range(8):
-            rows(1, m)
-
-    for m in range(8):
-        rows(0, m)
 
 
 def backward_kernel(levels_ref, recv_ref, out_ref, held):
@@ -164,8 +160,9 @@
                 for b in range(2):
                     covered, slot = cover_of(offsets, b, c, d)
                     for half in range(2):
-                        part = recv_ref[half * 8 + m, slot]
-                        parts.append(jnp.where(covered == 1, part, 0.0))
+                        for group in range(4):
+                            part = recv_ref[group, half * 8 + m, slot]
+                            parts.append(jnp.where(covered == 1, part, 0.0))
                 columns.append(jnp.concatenate(parts, axis=0))
             held[c * 8 + m] = rows_product(row, jnp.concatenate(columns, axis=1))
 
@@ -218,7 +215,7 @@
     weight_ref[...] = jnp.broadcast_to(total, (16, 128))
 
 
-def exchange_kernel(levels_ref, send_ref, out_ref, *scratch):
+def exchange_kernel(levels_ref, x_ref, out_ref, *scratch):
     (
         r1,
         acc,
@@ -245,6 +242,9 @@
         sendf,
         recvf,
         own,
+        send_ref,
+        held,
+        blocks_ref,
     ) = [scratch[4 * i : 4 * i + 4] for i in range(5)] + list(scratch[20:])
     half = lax.axis_index("half")
     line = lax.axis_index("grid")
@@ -286,10 +286,20 @@
     lax.fori_loop(1, 16, greet_group, 0)
     lax.fori_loop(1, 32, greet_dom, 0)
     lax.fori_loop(0, 8, greet_twin, 0)
+    offsets = offsets_of(levels_ref, me)
+    lower(offsets, x_ref, held, blocks_ref)
+    places = [blocks_of(offsets, slot) for slot in range(8)]
+
+    def pack(c):
+        def one(target, _):
+            for slot in range(8):
+                send_ref[c, target, slot] = blocks_ref[target, places[slot], pl.ds(8 * c, 8), :]
+            return 0
+
+        lax.fori_loop(0, 16, one, 0)
+
+    pack(0)
     pl.semaphore_wait(barrier, 54)
-
-    def rows(c):
-        return pl.ds(8 * c, 8)
 
     def sized(key, act):
         for option in range(3):
@@ -300,7 +310,7 @@
 
     def copy1(c, source, peer, count):
         return pltpu.make_async_remote_copy(
-            src_ref=send_ref.at[peer, pl.ds(0, count), rows(c)],
+            src_ref=send_ref.at[c, peer, pl.ds(0, count)],
             dst_ref=r1[c].at[source, pl.ds(0, count)],
             send_sem=send1.at[c, peer],
             recv_sem=recv1.at[c, source],
@@ -330,7 +340,7 @@
     def relay(way, c):
         target = {"half": 1 - half} if way == 0 else {"half": 1 - half, "dom": twin}
         return pltpu.make_async_remote_copy(
-            src_ref=send_ref.at[pl.ds(8 - 8 * way, 8), pl.ds(6, 2), rows(c)],
+            src_ref=send_ref.at[c, pl.ds(8 - 8 * way, 8), pl.ds(6, 2)],
             dst_ref=relayed[way][c],
             send_sem=sendr.at[way, c],
             recv_sem=recvr.at[way, c],
@@ -372,14 +382,25 @@
 
         lax.fori_loop(1, 16, one, 0)
 
+    def send(c):
+        @pl.when(gives)
+        def _():
+            for way in range(2):
+                relay(way, c).start()
+
+        start1(c)
+
+    send(0)
+    pack(1)
+    send(1)
+    pack(2)
+    pack(3)
+
     @pl.when(gives)
     def _():
-        for c in range(4):
+        for c in range(2, 4):
             for way in range(2):
                 relay(way, c).start()
-
-    start1(0)
-    start1(1)
 
     weigh(levels_ref, weight_ref)
     near = 1 - far
@@ -389,7 +410,7 @@
         grid = i // 8
         place = i % 8
         offsets = offsets_of(levels_ref, grid)
-        first, second, third, fourth = offsets
+        first = offsets[0]
         covered, slot = cover_of(offsets, place // 4, place // 2 % 2, place % 2)
         is_two = jnp.where(first == 2, 1, 0)
         is_one = jnp.where(first == 1, 1, 0) * near
@@ -398,11 +419,7 @@
         coef_ref[3 * i] = (covered * is_two).astype(jnp.float32)
         coef_ref[3 * i + 1] = (covered * is_one).astype(jnp.float32)
         coef_ref[3 * i + 2] = (covered * is_zero).astype(jnp.float32)
-        d_at = (place % 2) * fourth
-        rest = place + fourth * (place // 2 - place)
-        c_at = (rest % 2) * third
-        rest = rest + third * (rest // 2 - rest)
-        chosen = jnp.where(rest <= second, rest * 4 + c_at * 2 + d_at, 0)
+        chosen = blocks_of(offsets, place)
         pick_ref[i] = chosen * 3 + is_one + 2 * is_zero
         return 0
 
@@ -443,8 +460,8 @@
 
     def copy4(c, source, peer, count):
         return pltpu.make_async_remote_copy(
-            src_ref=s2.at[peer, pl.ds(0, count), rows(c)],
-            dst_ref=out_ref.at[source, pl.ds(0, count), rows(c)],
+            src_ref=s2.at[c, peer, pl.ds(0, count)],
+            dst_ref=out_ref.at[c, source, pl.ds(0, count)],
             send_sem=send4.at[c, peer],
             recv_sem=recv4.at[c, source],
             device_id={"half": peer // 8, "grid": peer % 8},
@@ -498,7 +515,7 @@
 
     def summed(c):
         def keep(slot, _):
-            r1[c][me, slot] = send_ref[me, slot, rows(c), :]
+            r1[c][me, slot] = send_ref[c, me, slot]
             return 0
 
         lax.fori_loop(0, 8, keep, 0)
@@ -584,7 +601,7 @@
 
         def fill(peer):
             for slot in range(8):
-                s2[peer, slot, rows(c), :] = r3[c][pick_ref[peer * 8 + slot]]
+                s2[c, peer, slot] = r3[c][pick_ref[peer * 8 + slot]]
 
         def start4(k, _):
             peer = (me + k) % 16
@@ -618,7 +635,7 @@
     deliver(2)
     deliver(3)
 
-    home = pltpu.make_async_copy(s2.at[me], out_ref.at[me], own)
+    home = pltpu.make_async_copy(s2.at[:, me], out_ref.at[:, me], own)
     home.start()
 
     for c in range(4):
@@ -678,12 +695,12 @@
     lax.fori_loop(1, 32, sent3, 0)
 
 
-def exchange(levels, packed):
+def exchange(levels, values):
     dma = pltpu.SemaphoreType.DMA
     f32 = jnp.float32
     return pl.pallas_call(
         exchange_kernel,
-        out_shape=jax.ShapeDtypeStruct((16, 8, 32, 128), f32),
+        out_shape=jax.ShapeDtypeStruct((4, 16, 8, 8, 128), f32),
         in_specs=[
             pl.BlockSpec(memory_space=pltpu.SMEM),
             pl.BlockSpec(memory_space=pltpu.VMEM),
@@ -696,7 +713,7 @@
         + [
             pltpu.VMEM((32, 3, 8, 128), f32),
             pltpu.VMEM((32, 3, 8, 128), f32),
-            pltpu.VMEM((16, 8, 32, 128), f32),
+            pltpu.VMEM((4, 16, 8, 8, 128), f32),
             pltpu.VMEM((16, 128), f32),
             pltpu.SMEM((128,), jnp.int32),
             pltpu.SMEM((384,), f32),
@@ -714,11 +731,14 @@
             dma((2, 4, 8)),
             dma((4, 8)),
             dma,
+            pltpu.VMEM((4, 16, 8, 8, 128), f32),
+            pltpu.VMEM((24, 128, 256), f32),
+            pltpu.VMEM((16, 8, 32, 128), f32),
         ],
         compiler_params=pltpu.CompilerParams(
             collective_id=0, has_side_effects=True, vmem_limit_bytes=32 * 2**20
         ),
-    )(levels, packed)
+    )(levels, values)
 
 
 def local_call(kernel, levels, values, out_shape):
@@ -737,8 +757,7 @@
 
 def per_device(grids, levels):
     turned = levels.T
-    packed = local_call(forward_kernel, turned, grids.reshape(128, 4096), (16, 8, 32, 128))
-    received = exchange(turned, packed)
+    received = exchange(turned, grids.reshape(128, 4096))
     combined = local_call(backward_kernel, turned, received, (128, 4096))
     return combined.reshape(grids.shape)
 

time: 106 us -> 102 us (0.962)
  Pallas kernels: 102 us -> 98 us
    pallas_call x2 -> x1, Pallas kernels: 8.38 us -> 3.71 us  [local_call(): pl.pallas_call(kernel, out_shape=jax.ShapeDtypeStruct(out_shape, jnp.floa...]
where the time goes in v5:
time: 102 us; the launch traced here: 100 us
  Pallas kernels  98 us (96%)
  local copies, waits for them, and re-layouts  2.27 us (2%)
    pallas_call x1, Pallas kernels, exchange(): pl.pallas_call(exchange_kernel, out_shape=jax.ShapeDtypeStruct((4, 16, 8,...  94.3 us
    pallas_call x1, Pallas kernels, local_call(): pl.pallas_call(kernel, out_shape=jax.ShapeDtypeStruct(out_shape, jnp.floa...  3.71 us
    unnamed x4, local copies, waits for them, and re-layouts  2.27 us

profile of v5, /device:TPU:1, one launch (start us, length us, event | category | flops | bytes accessed | tf_op | source)
XLA Modules:
  0.0 100.3 jit_solution(11413358244036877838)
XLA Ops:
  0.0 0.0 copy-start
  0.0 1.6 %copy-done = f32[1,2,64,4096]{3,2,1,0:T(8,128)S(1)} copy-done((f32[1,2,64,4096]{3,2,1,0:T(8,128)S(1)}, f32[1,2,64,4096]{3,2,1,0:T(8,128)}, u32[]{:S(2)}) %copy-start) | copy-done | bytes 2097176
  1.6 0.0 copy-start.1
  1.6 0.7 copy-done.1
  2.3 94.3 %shard_map.28.recv_ref = f32[4,16,8,8,128]{4,3,2,1,0:T(8,128)S(1)} custom-call(s32[4,16]{1,0:T(4,128)S(1)} %bitcast.4, f32[128,4096]{1,0:T(8,128)S(1)} %bitcast.3), custom_call_target="tpu_custom_call" | custom-call | tf_op jit(solution)/shard_map/pallas_call | solution.py:701
  96.6 3.7 %shard_map.29 = f32[128,4096]{1,0:T(8,128)} custom-call(s32[4,16]{1,0:T(4,128)S(1)} %bitcast.5, f32[4,16,8,8,128]{4,3,2,1,0:T(8,128)S(1)} %shard_map.28.recv_ref), custom_call_target="tpu_custom_call" | custom-call | tf_op jit(solution)/shard_map/pallas_call | solution.py:745
Async XLA Ops:
  0.0 1.6 %copy-start = (f32[1,2,64,4096]{3,2,1,0:T(8,128)S(1)}, f32[1,2,64,4096]{3,2,1,0:T(8,128)}, u32[]{:S(2)}) copy-start(f32[1,2,64,4096]{3,2,1,0:T(8,128)} %param.2) | copy-start | bytes 6291460
  1.6 0.7 copy-start.1

commit v6 on v5

--- a/solution.py
+++ b/solution.py
@@ -220,8 +220,7 @@
         r1,
         acc,
         r3,
-        first_relay,
-        second_relay,
+        relayed,
         r2,
         o2,
         s2,
@@ -245,16 +244,15 @@
         send_ref,
         held,
         blocks_ref,
-    ) = [scratch[4 * i : 4 * i + 4] for i in range(5)] + list(scratch[20:])
+        here,
+    ) = [scratch[4 * i : 4 * i + 4] for i in range(4)] + list(scratch[16:])
     half = lax.axis_index("half")
     line = lax.axis_index("grid")
     me = half * 8 + line
     dom = lax.axis_index("dom")
     far = dom // 16
-    twin = dom + 2 - 4 * (dom // 2 % 2)
     mine = dom % 4
     my_e = dom // 4
-    relayed = (first_relay, second_relay)
 
     for s in range(8):
         r2[s, 2] = jnp.zeros((8, 128), jnp.float32)
@@ -268,24 +266,34 @@
         )
         return 0
 
-    def greet_dom(k, _):
+    def greet_near(k, _):
         pl.semaphore_signal(
             barrier, inc=1, device_id={"dom": (dom + k) % 32}, device_id_type=MESH
         )
         return 0
 
-    def greet_twin(k, _):
+    def greet_far(k, _):
         pl.semaphore_signal(
-            barrier,
-            inc=1,
-            device_id={"half": 1 - half, "grid": k, "dom": twin},
-            device_id_type=MESH,
+            barrier, inc=1, device_id={"dom": 16 + (dom + k) % 16}, device_id_type=MESH
         )
         return 0
 
+    def answer(k, _):
+        pl.semaphore_signal(
+            here, inc=1, device_id={"dom": (dom + k) % 16}, device_id_type=MESH
+        )
+        return 0
+
     lax.fori_loop(1, 16, greet_group, 0)
-    lax.fori_loop(1, 32, greet_dom, 0)
-    lax.fori_loop(0, 8, greet_twin, 0)
+
+    @pl.when(far == 0)
+    def _():
+        lax.fori_loop(1, 32, greet_near, 0)
+
+    @pl.when(far == 1)
+    def _():
+        lax.fori_loop(1, 16, greet_far, 0)
+
     offsets = offsets_of(levels_ref, me)
     lower(offsets, x_ref, held, blocks_ref)
     places = [blocks_of(offsets, slot) for slot in range(8)]
@@ -299,7 +307,16 @@
         lax.fori_loop(0, 16, one, 0)
 
     pack(0)
-    pl.semaphore_wait(barrier, 54)
+
+    @pl.when(far == 0)
+    def _():
+        pl.semaphore_wait(barrier, 30)
+
+    @pl.when(far == 1)
+    def _():
+        pl.semaphore_wait(barrier, 46)
+        lax.fori_loop(0, 16, answer, 0)
+
 
     def sized(key, act):
         for option in range(3):
@@ -318,18 +335,15 @@
             device_id_type=MESH,
         )
 
-    def shared(source_half, across, act):
-        key = source_half + far
-
-        @pl.when((key == 0) & across)
+    def shared(source, owner_at, act):
+        key = source // 8 + far
+        direct = (owner_at // 8 == 0) | (source % 8 == owner_at % 8)
+
+        @pl.when((key == 0) & direct)
         def _():
             act(8)
 
-        @pl.when((key == 0) & jnp.logical_not(across))
-        def _():
-            act(6)
-
-        @pl.when(key == 1)
+        @pl.when(((key == 0) & jnp.logical_not(direct)) | (key == 1))
         def _():
             act(4)
 
@@ -337,25 +351,23 @@
         def _():
             act(2)
 
-    def relay(way, c):
-        target = {"half": 1 - half} if way == 0 else {"half": 1 - half, "dom": twin}
+    def relay(c):
         return pltpu.make_async_remote_copy(
-            src_ref=send_ref.at[c, pl.ds(8 - 8 * way, 8), pl.ds(6, 2)],
-            dst_ref=relayed[way][c],
-            send_sem=sendr.at[way, c],
-            recv_sem=recvr.at[way, c],
-            device_id=target,
+            src_ref=send_ref.at[c, pl.ds(8, 8), pl.ds(4, 4)],
+            dst_ref=relayed[c],
+            send_sem=sendr.at[c],
+            recv_sem=recvr.at[c],
+            device_id={"half": 1 - half},
             device_id_type=MESH,
         )
 
-    def forward(way, c, source, to):
-        target = {"grid": to} if way == 0 else {"half": 1 - half, "grid": to, "dom": twin}
+    def forward(c, source, to):
         return pltpu.make_async_remote_copy(
-            src_ref=relayed[way][c].at[to],
-            dst_ref=r1[c].at[source, pl.ds(6, 2)],
-            send_sem=sendf.at[way, c, to],
+            src_ref=relayed[c].at[to],
+            dst_ref=r1[c].at[source, pl.ds(4, 4)],
+            send_sem=sendf.at[c, to],
             recv_sem=recvf.at[c, source],
-            device_id=target,
+            device_id={"grid": to},
             device_id_type=MESH,
         )
 
@@ -365,19 +377,18 @@
     def pass_on(c):
         @pl.when(takes)
         def _():
-            for way in range(2):
-                relay(way, c).wait_recv()
-
-                def one(k, _):
-                    forward(way, c, line, (line + k) % 8).start()
-                    return 0
-
-                lax.fori_loop(1, 8, one, 0)
+            relay(c).wait_recv()
+
+            def one(k, _):
+                forward(c, line, (line + k) % 8).start()
+                return 0
+
+            lax.fori_loop(1, 8, one, 0)
 
     def start1(c):
         def one(k, _):
             peer = (me + k) % 16
-            shared(half, peer % 8 == line, lambda count: copy1(c, me, peer, count).start())
+            shared(me, peer, lambda count: copy1(c, me, peer, count).start())
             return 0
 
         lax.fori_loop(1, 16, one, 0)
@@ -385,8 +396,7 @@
     def send(c):
         @pl.when(gives)
         def _():
-            for way in range(2):
-                relay(way, c).start()
+            relay(c).start()
 
         start1(c)
 
@@ -399,8 +409,7 @@
     @pl.when(gives)
     def _():
         for c in range(2, 4):
-            for way in range(2):
-                relay(way, c).start()
+            relay(c).start()
 
     weigh(levels_ref, weight_ref)
     near = 1 - far
@@ -502,12 +511,11 @@
     def arrive(c):
         def wait1(k, _):
             source = (me + 16 - k) % 16
-            across = source % 8 == line
-            shared(source // 8, across, lambda count: copy1(c, source, source, count).wait_recv())
-
-            @pl.when((source // 8 + far == 0) & jnp.logical_not(across))
-            def _():
-                forward(0, c, source % 8, source % 8).wait_recv()
+            shared(source, me, lambda count: copy1(c, source, source, count).wait_recv())
+
+            @pl.when((source // 8 == 0) & takes & (source % 8 != line))
+            def _():
+                forward(c, source % 8, source % 8).wait_recv()
 
             return 0
 
@@ -613,28 +621,32 @@
         fill(me)
 
     pass_on(0)
+    start1(2)
     pass_on(1)
     arrive(0)
-    start1(2)
+    start1(3)
+
+    @pl.when(far == 0)
+    def _():
+        pl.semaphore_wait(here, 16)
+
     summed(0)
     pass_on(2)
     owned(0)
+    pass_on(3)
     arrive(1)
-    start1(3)
     summed(1)
-    pass_on(3)
     owned(1)
     arrive(2)
     summed(2)
+    deliver(0)
     owned(2)
-    deliver(0)
+    deliver(1)
     arrive(3)
     summed(3)
-    deliver(1)
     owned(3)
     deliver(2)
     deliver(3)
-
     home = pltpu.make_async_copy(s2.at[:, me], out_ref.at[:, me], own)
     home.start()
 
@@ -652,7 +664,7 @@
     def sent_group(k, _):
         peer = (me + k) % 16
         for c in range(4):
-            shared(half, peer % 8 == line, lambda count: copy1(c, me, peer, count).wait_send())
+            shared(me, peer, lambda count: copy1(c, me, peer, count).wait_send())
             sized(peer // 8 + far, lambda count: copy4(c, me, peer, count).wait_send())
         return 0
 
@@ -661,15 +673,13 @@
     @pl.when(gives)
     def _():
         for c in range(4):
-            for way in range(2):
-                relay(way, c).wait_send()
+            relay(c).wait_send()
 
     @pl.when(takes)
     def _():
         def passed(k, _):
             for c in range(4):
-                for way in range(2):
-                    forward(way, c, line, (line + k) % 8).wait_send()
+                forward(c, line, (line + k) % 8).wait_send()
             return 0
 
         lax.fori_loop(1, 8, passed, 0)
@@ -709,7 +719,7 @@
         scratch_shapes=[pltpu.VMEM((16, 8, 8, 128), f32)] * 4
         + [pltpu.VMEM((8, 3, 8, 128), f32)] * 4
         + [pltpu.VMEM((24, 8, 128), f32)] * 4
-        + [pltpu.VMEM((8, 2, 8, 128), f32)] * 8
+        + [pltpu.VMEM((8, 4, 8, 128), f32)] * 4
         + [
             pltpu.VMEM((32, 3, 8, 128), f32),
             pltpu.VMEM((32, 3, 8, 128), f32),
@@ -726,14 +736,15 @@
             dma((4, 8)),
             dma((4, 16)),
             dma((4, 16)),
-            dma((2, 4)),
-            dma((2, 4)),
-            dma((2, 4, 8)),
+            dma((4,)),
+            dma((4,)),
+            dma((4, 8)),
             dma((4, 8)),
             dma,
             pltpu.VMEM((4, 16, 8, 8, 128), f32),
             pltpu.VMEM((24, 128, 256), f32),
             pltpu.VMEM((16, 8, 32, 128), f32),
+            pltpu.SemaphoreType.REGULAR,
         ],
         compiler_params=pltpu.CompilerParams(
             collective_id=0, has_side_effects=True, vmem_limit_bytes=32 * 2**20

time: 102 us -> 98.1 us (0.962); the launches traced: 100 us -> 97.9 us
  Pallas kernels: 98 us -> 95.6 us
    pallas_call x1, Pallas kernels: 94.3 us -> 91.9 us  [exchange(): pl.pallas_call(exchange_kernel, out_shape=jax.ShapeDtypeStruct((4, 16, 8,...]
where the time goes in v6:
time: 98.1 us; the launch traced here: 97.9 us
  Pallas kernels  95.6 us (97%)
  local copies, waits for them, and re-layouts  2.27 us (2%)
    pallas_call x1, Pallas kernels, exchange(): pl.pallas_call(exchange_kernel, out_shape=jax.ShapeDtypeStruct((4, 16, 8,...  91.9 us
    pallas_call x1, Pallas kernels, local_call(): pl.pallas_call(kernel, out_shape=jax.ShapeDtypeStruct(out_shape, jnp.floa...  3.71 us
    unnamed x4, local copies, waits for them, and re-layouts  2.27 us

profile of v6, /device:TPU:1, one launch (start us, length us, event | category | flops | bytes accessed | tf_op | source)
XLA Modules:
  0.0 97.9 jit_solution(6667755688211133828)
XLA Ops:
  0.0 0.0 copy-start
  0.0 1.6 %copy-done = f32[1,2,64,4096]{3,2,1,0:T(8,128)S(1)} copy-done((f32[1,2,64,4096]{3,2,1,0:T(8,128)S(1)}, f32[1,2,64,4096]{3,2,1,0:T(8,128)}, u32[]{:S(2)}) %copy-start) | copy-done | bytes 2097176
  1.6 0.0 copy-start.1
  1.6 0.7 copy-done.1
  2.3 91.9 %shard_map.28.recv_ref = f32[4,16,8,8,128]{4,3,2,1,0:T(8,128)S(1)} custom-call(s32[4,16]{1,0:T(4,128)S(1)} %bitcast.4, f32[128,4096]{1,0:T(8,128)S(1)} %bitcast.3), custom_call_target="tpu_custom_call" | custom-call | tf_op jit(solution)/shard_map/pallas_call | solution.py:711
  94.2 3.7 %shard_map.29 = f32[128,4096]{1,0:T(8,128)} custom-call(s32[4,16]{1,0:T(4,128)S(1)} %bitcast.5, f32[4,16,8,8,128]{4,3,2,1,0:T(8,128)S(1)} %shard_map.28.recv_ref), custom_call_target="tpu_custom_call" | custom-call | tf_op jit(solution)/shard_map/pallas_call | solution.py:756
Async XLA Ops:
  0.0 1.6 %copy-start = (f32[1,2,64,4096]{3,2,1,0:T(8,128)S(1)}, f32[1,2,64,4096]{3,2,1,0:T(8,128)}, u32[]{:S(2)}) copy-start(f32[1,2,64,4096]{3,2,1,0:T(8,128)} %param.2) | copy-start | bytes 6291460
  1.6 0.7 copy-start.1

commit v7 on v6

--- a/solution.py
+++ b/solution.py
@@ -385,9 +385,14 @@
 
             lax.fori_loop(1, 8, one, 0)
 
+    def ordered(k):
+        step = (k - 1) // 2
+        away = 4 + step // 2 - (step % 2) * (1 + 2 * (step // 2))
+        return (half + k % 2) % 2 * 8 + (line + away) % 8
+
     def start1(c):
         def one(k, _):
-            peer = (me + k) % 16
+            peer = ordered(k)
             shared(me, peer, lambda count: copy1(c, me, peer, count).start())
             return 0
 
@@ -612,7 +617,7 @@
                 s2[c, peer, slot] = r3[c][pick_ref[peer * 8 + slot]]
 
         def start4(k, _):
-            peer = (me + k) % 16
+            peer = ordered(k)
             fill(peer)
             sized(peer // 8 + far, lambda count: copy4(c, me, peer, count).start())
             return 0
@@ -632,21 +637,22 @@
 
     summed(0)
     pass_on(2)
+    pass_on(3)
     owned(0)
-    pass_on(3)
     arrive(1)
     summed(1)
+    deliver(0)
     owned(1)
     arrive(2)
     summed(2)
-    deliver(0)
+    deliver(1)
     owned(2)
-    deliver(1)
     arrive(3)
     summed(3)
+    deliver(2)
     owned(3)
-    deliver(2)
     deliver(3)
+
     home = pltpu.make_async_copy(s2.at[:, me], out_ref.at[:, me], own)
     home.start()
 

time: 98.1 us -> 95.7 us (0.976)
  Pallas kernels: 95.6 us -> 93.5 us
    pallas_call x1, Pallas kernels: 91.9 us -> 89.8 us  [exchange(): pl.pallas_call(exchange_kernel, out_shape=jax.ShapeDtypeStruct((4, 16, 8,...]
where the time goes in v7:
time: 95.7 us
  Pallas kernels  93.5 us (98%)
  local copies, waits for them, and re-layouts  2.27 us (2%)
    pallas_call x1, Pallas kernels, exchange(): pl.pallas_call(exchange_kernel, out_shape=jax.ShapeDtypeStruct((4, 16, 8,...  89.8 us
    pallas_call x1, Pallas kernels, local_call(): pl.pallas_call(kernel, out_shape=jax.ShapeDtypeStruct(out_shape, jnp.floa...  3.7 us
    unnamed x4, local copies, waits for them, and re-layouts  2.27 us

profile of v7, /device:TPU:1, one launch (start us, length us, event | category | flops | bytes accessed | tf_op | source)
XLA Modules:
  0.0 95.7 jit_solution(11762858400633473907)
XLA Ops:
  0.0 0.0 copy-start
  0.0 1.6 %copy-done = f32[1,2,64,4096]{3,2,1,0:T(8,128)S(1)} copy-done((f32[1,2,64,4096]{3,2,1,0:T(8,128)S(1)}, f32[1,2,64,4096]{3,2,1,0:T(8,128)}, u32[]{:S(2)}) %copy-start) | copy-done | bytes 2097176
  1.6 0.0 copy-start.1
  1.6 0.7 copy-done.1
  2.3 89.8 %shard_map.28.recv_ref = f32[4,16,8,8,128]{4,3,2,1,0:T(8,128)S(1)} custom-call(s32[4,16]{1,0:T(4,128)S(1)} %bitcast.4, f32[128,4096]{1,0:T(8,128)S(1)} %bitcast.3), custom_call_target="tpu_custom_call" | custom-call | tf_op jit(solution)/shard_map/pallas_call | solution.py:717
  92.0 3.7 %shard_map.29 = f32[128,4096]{1,0:T(8,128)} custom-call(s32[4,16]{1,0:T(4,128)S(1)} %bitcast.5, f32[4,16,8,8,128]{4,3,2,1,0:T(8,128)S(1)} %shard_map.28.recv_ref), custom_call_target="tpu_custom_call" | custom-call | tf_op jit(solution)/shard_map/pallas_call | solution.py:762
Async XLA Ops:
  0.0 1.6 %copy-start = (f32[1,2,64,4096]{3,2,1,0:T(8,128)S(1)}, f32[1,2,64,4096]{3,2,1,0:T(8,128)}, u32[]{:S(2)}) copy-start(f32[1,2,64,4096]{3,2,1,0:T(8,128)} %param.2) | copy-start | bytes 6291460
  1.6 0.7 copy-start.1

commit v8 on v7

--- a/solution.py
+++ b/solution.py
@@ -411,10 +411,6 @@
     pack(2)
     pack(3)
 
-    @pl.when(gives)
-    def _():
-        for c in range(2, 4):
-            relay(c).start()
 
     weigh(levels_ref, weight_ref)
     near = 1 - far
@@ -626,10 +622,10 @@
         fill(me)
 
     pass_on(0)
-    start1(2)
+    send(2)
     pass_on(1)
     arrive(0)
-    start1(3)
+    send(3)
 
     @pl.when(far == 0)
     def _():

time: 95.7 us -> 95.8 us (level)
  no operation moved by 1% of the time
where the time goes in v8:
time: 95.8 us
  Pallas kernels  93.6 us (98%)
  local copies, waits for them, and re-layouts  2.27 us (2%)
    pallas_call x1, Pallas kernels, exchange(): pl.pallas_call(exchange_kernel, out_shape=jax.ShapeDtypeStruct((4, 16, 8,...  89.8 us
    pallas_call x1, Pallas kernels, local_call(): pl.pallas_call(kernel, out_shape=jax.ShapeDtypeStruct(out_shape, jnp.floa...  3.72 us
    unnamed x4, local copies, waits for them, and re-layouts  2.27 us

profile of v8, /device:TPU:1, one launch (start us, length us, event | category | flops | bytes accessed | tf_op | source)
XLA Modules:
  0.0 95.8 jit_solution(8994989196990540881)
XLA Ops:
  0.0 0.0 copy-start
  0.0 1.6 %copy-done = f32[1,2,64,4096]{3,2,1,0:T(8,128)S(1)} copy-done((f32[1,2,64,4096]{3,2,1,0:T(8,128)S(1)}, f32[1,2,64,4096]{3,2,1,0:T(8,128)}, u32[]{:S(2)}) %copy-start) | copy-done | bytes 2097176
  1.6 0.0 copy-start.1
  1.6 0.7 copy-done.1
  2.3 89.8 %shard_map.28.recv_ref = f32[4,16,8,8,128]{4,3,2,1,0:T(8,128)S(1)} custom-call(s32[4,16]{1,0:T(4,128)S(1)} %bitcast.4, f32[128,4096]{1,0:T(8,128)S(1)} %bitcast.3), custom_call_target="tpu_custom_call" | custom-call | tf_op jit(solution)/shard_map/pallas_call | solution.py:713
  92.1 3.7 %shard_map.29 = f32[128,4096]{1,0:T(8,128)} custom-call(s32[4,16]{1,0:T(4,128)S(1)} %bitcast.5, f32[4,16,8,8,128]{4,3,2,1,0:T(8,128)S(1)} %shard_map.28.recv_ref), custom_call_target="tpu_custom_call" | custom-call | tf_op jit(solution)/shard_map/pallas_call | solution.py:758
Async XLA Ops:
  0.0 1.6 %copy-start = (f32[1,2,64,4096]{3,2,1,0:T(8,128)S(1)}, f32[1,2,64,4096]{3,2,1,0:T(8,128)}, u32[]{:S(2)}) copy-start(f32[1,2,64,4096]{3,2,1,0:T(8,128)} %param.2) | copy-start | bytes 6291460
  1.6 0.7 copy-start.1
